TPU v7x, 256 devices: a whole 4x4x8 slice. The times are simulated.
256 devices in a mesh: layer: 8 (over x, y_hi), latent: 16 (over z, core), dp: 2 (over y_lo).
Axes of the slice: x: 4, y: 4 (y_hi: 2, y_lo: 2; y = y_hi * 2 + y_lo), z: 8, core: 2. Of those that a mesh axis runs over, the one named last changes fastest.
Arguments:
- inputs: bfloat16 [512, 8, 2560], P('dp', 'layer'), may hold values from -6 to 6
- targets: bfloat16 [512, 8, 2560], P(('latent', 'dp'), 'layer'), may hold values from -6 to 6
- w_enc: bfloat16 [8, 2560, 8192], P('layer', None, ('latent', 'dp')), may hold values from -0.125 to 0.125
- b_enc: float32 [8, 8192], P('layer', ('latent', 'dp')), may hold values from -0.75 to 0.25
- w_dec: bfloat16 [8, 4, 8192, 2560], P('layer', None, ('latent', 'dp')), may hold values from -0.0625 to 0.0625
Outputs:
- grad_dec: bfloat16 [8, 4, 8192, 2560], P('layer', None, ('latent', 'dp'))
- grad_latents: float32 [512, 8, 8192], P(None, 'layer', ('latent', 'dp'))
All inputs are finite; a program needn't handle non-finite values.
Results may differ from a plain program's by a relative error of at most 0.0044.
Values may be sent and summed in bfloat16 or wider, within the bound.
No kernel may reach another device: no remote copies, remote signals or barrier semaphores. Data moves between devices by JAX's collectives and lax.ppermute only.
A program may use at most 64 MiB of HBM per device.

v0:
```python
import math

import jax
import jax.numpy as jnp
from jax import lax
from jax.sharding import PartitionSpec as P

SPARSITY = 1.0
EPSILON = 1e-06


def shifted_2(block, axis, distance):
    devices = range(lax.axis_size(axis))
    route = [(i - distance, i) for i in devices if i - distance in devices]
    return lax.ppermute(block, axis, route)


def shards(inputs, targets, w_enc, b_enc, w_dec):
    reach_count = w_dec.shape[1]
    enc_weight = w_enc[0]
    enc_bias = b_enc[0]
    preact = (
        jnp.dot(
            lax.all_gather(inputs, "dp", axis=0, tiled=True)[:, 0],
            enc_weight,
            preferred_element_type=jnp.float32,
        )
        + enc_bias
    )
    local_latents = jnp.maximum(preact, 0.0).astype(jnp.bfloat16)
    token_count = local_latents.shape[0]
    sources = [local_latents]
    for distance in range(1, reach_count):
        sources.append(shifted_2(local_latents, "layer", distance))
    weights = w_dec[0]
    channels = weights.shape[2]
    loss_scale = 1.0 / math.sqrt(token_count)
    penalty = SPARSITY * loss_scale
    row_total = targets.shape[0]
    own_targets = targets[:, 0].astype(jnp.float32)
    running = jnp.zeros((token_count, channels), jnp.float32)
    for project_distance in range(reach_count):
        block = sources[project_distance]
        running = running + jnp.dot(
            block, weights[project_distance], preferred_element_type=jnp.float32
        )
    partial_value = running
    offset = lax.axis_index(("latent", "dp")) * row_total
    shifted = lax.dynamic_slice_in_dim(partial_value, offset, row_total, 0) - own_targets
    partial_value = lax.dynamic_update_slice_in_dim(partial_value, shifted, offset, 0)
    misfit = lax.psum(partial_value, ("latent", "dp"))
    grad_out = (misfit * loss_scale).astype(jnp.bfloat16)
    column_norms = jnp.sqrt(jnp.sum(jnp.square(weights.astype(jnp.float32)), axis=2) + EPSILON)
    pieces = []
    upward = None
    for distance in range(reach_count):
        source = sources[distance]
        contrib = lax.dot_general(
            source, grad_out, (((0,), (0,)), ((), ())), preferred_element_type=jnp.float32
        )
        latent_mass = jnp.sum(source.astype(jnp.float32), axis=0)
        contrib = contrib + (penalty * latent_mass / column_norms[distance])[:, None] * weights[
            distance
        ].astype(jnp.float32)
        pieces.append(contrib.astype(jnp.bfloat16))
        back_term = lax.dot_general(
            grad_out,
            weights[distance],
            (((1,), (1,)), ((), ())),
            preferred_element_type=jnp.float32,
        )
        back_term = back_term + penalty * column_norms[distance][None, :]
        if distance == 0:
            upward = back_term
        else:
            upward = upward + shifted_2(back_term.astype(jnp.bfloat16), "layer", -distance).astype(
                back_term.dtype
            )
    grad_dec = jnp.stack(pieces)[None]
    return (grad_dec, upward[:, None, :])


def solution(mesh):
    placed = (
        P("dp", "layer", None),
        P(("latent", "dp"), "layer", None),
        P("layer", None, ("latent", "dp")),
        P("layer", ("latent", "dp")),
        P("layer", None, ("latent", "dp"), None),
    )
    return jax.shard_map(
        shards,
        mesh=mesh,
        in_specs=placed,
        out_specs=(P("layer", None, ("latent", "dp"), None), P(None, "layer", ("latent", "dp"))),
        check_vma=False,
    )
```

profile of v0, /device:TPU:38, one launch (start us, length us, event | category | flops | bytes accessed | tf_op | source)
XLA Modules:
  0.0 376.2 jit_solution(15223629919855892046)
XLA Ops:
  8.0 48.5 %all-gather.2.cloned.1.call-done = bf16[512,1,2560]{2,0,1:T(8,128)(2,1)} async-done(((bf16[256,1,2560]{2,0,1:T(8,128)(2,1)}), bf16[512,1,2560]{2,0,1:T(8,128)(2,1)}) %all-gather.2.cloned.1.call-update) | async-done | bytes 2621456 | tf_op jit(solution)/shard_map/all_gather | solution.py:24
  56.5 2.7 convert_reduce_fusion.3
  59.3 1.3 collective-permute-start.1
  60.6 4.6 %collective-permute-start = (bf16[512,256]{1,0:T(8,128)(2,1)S(1)}, bf16[512,256]{1,0:T(8,128)(2,1)S(1)}, u32[]{:S(2)}, u32[]{:S(2)}) collective-permute-start(bf16[512,256]{1,0:T(8,128)(2,1)S(1)} %get-tuple-element.13), channel_id=1, source_target_pairs={{0,32},{32,64},{64,96},{96,128},{128,160},{160,192},{192,224},{1,3... | collective-permute-start | bytes 786440 | tf_op jit(solution)/shard_map/ppermute | solution.py:15
  65.2 1.3 collective-permute-start.2
  67.3 1.9 collective-permute-done.1
  70.0 12.5 %collective-permute-done = bf16[512,256]{1,0:T(8,128)(2,1)S(1)} collective-permute-done((bf16[512,256]{1,0:T(8,128)(2,1)S(1)}, bf16[512,256]{1,0:T(8,128)(2,1)S(1)}, u32[]{:S(2)}, u32[]{:S(2)}) %collective-permute-start) | collective-permute-done | bytes 262176 | tf_op jit(solution)/shard_map/ppermute | solution.py:15
  83.5 3.5 add_add_fusion
  87.0 1.6 fusion.75
  88.6 3.6 multiply_reduce_fusion
  92.5 247.5 %all-reduce.2.cloned.1.call-done = f32[512,2560]{1,0:T(8,128)} async-done(((f32[512,2560]{1,0:T(8,128)}), f32[512,2560]{1,0:T(8,128)}) %all-reduce.2.cloned.1.call-update) | async-done | bytes 5242896 | tf_op jit(solution)/shard_map/psum | solution.py:51
  340.0 3.1 multiply_convert_fusion
  343.1 2.3 fusion.57
  345.5 5.0 %collective-permute-start.3 = (bf16[512,256]{1,0:T(8,128)(2,1)S(1)}, bf16[512,256]{1,0:T(8,128)(2,1)S(1)}, u32[]{:S(2)}, u32[]{:S(2)}) collective-permute-start(bf16[512,256]{1,0:T(8,128)(2,1)S(1)} %fusion.57), channel_id=1, source_target_pairs={{32,0},{64,32},{96,64},{128,96},{160,128},{192,160},{224,192},{33,... | collective-permute-start | bytes 786440 | tf_op jit(solution)/shard_map/ppermute | solution.py:15
  350.5 2.3 fusion.54
  352.8 2.6 collective-permute-start.4
  356.3 3.5 collective-permute-start.5
  359.9 0.9 fusion.7
  360.8 0.9 fusion.5
  361.7 0.9 fusion.6
  362.6 0.9 fusion.4
  363.6 2.9 maximum_bitcast_fusion
  367.1 0.9 add_bitcast_fusion
  368.0 1.3 copy.7
  (32 shorter events, 5.1 us)
Async XLA Ops:
  7.2 49.3 %copy-start = (bf16[1,2560,256]{2,1,0:T(8,128)(2,1)S(1)}, bf16[1,2560,256]{2,1,0:T(8,128)(2,1)}, u32[]{:S(2)}) copy-start(bf16[1,2560,256]{2,1,0:T(8,128)(2,1)} %param.7) | copy-start | bytes 3932164
  7.2 49.3 %all-gather.2.cloned.1.call-start = ((), (), s32[]{:S(2)}) async-start(), calls=%async_computation | async-start | bytes 3932160 | tf_op jit(solution)/shard_map/all_gather | solution.py:24
  7.9 332.1 %all-reduce.2.cloned.1.call-start = ((), (), s32[]{:S(2)}) async-start(), calls=%async_computation.1 | async-start | bytes 10485760 | tf_op jit(solution)/shard_map/psum | solution.py:51
  56.5 10.0 %copy-start.1 = (bf16[1,4,256,2560]{3,2,1,0:T(8,128)(2,1)S(1)}, bf16[1,4,256,2560]{3,2,1,0:T(8,128)(2,1)}, u32[]{:S(2)}) copy-start(bf16[1,4,256,2560]{3,2,1,0:T(8,128)(2,1)} %param.9) | copy-start | bytes 15728644
  59.3 9.9 %collective-permute-start.1 = (bf16[512,256]{1,0:T(8,128)(2,1)S(1)}, bf16[512,256]{1,0:T(8,128)(2,1)S(1)}, u32[]{:S(2)}, u32[]{:S(2)}) collective-permute-start(bf16[512,256]{1,0:T(8,128)(2,1)S(1)} %get-tuple-element.13), channel_id=1, source_target_pairs={{0,64},{32,96},{64,128},{96,160},{128,192},{160,224},{1,65},{33,97... | collective-permute-start | bytes 786440 | tf_op jit(solution)/shard_map/ppermute | solution.py:15
  60.6 22.0 %collective-permute-start = (bf16[512,256]{1,0:T(8,128)(2,1)S(1)}, bf16[512,256]{1,0:T(8,128)(2,1)S(1)}, u32[]{:S(2)}, u32[]{:S(2)}) collective-permute-start(bf16[512,256]{1,0:T(8,128)(2,1)S(1)} %get-tuple-element.13), channel_id=1, source_target_pairs={{0,32},{32,64},{64,96},{96,128},{128,160},{160,192},{192,224},{1,3... | collective-permute-start | bytes 786440 | tf_op jit(solution)/shard_map/ppermute | solution.py:15
  65.2 18.3 %collective-permute-start.2 = (bf16[512,256]{1,0:T(8,128)(2,1)S(1)}, bf16[512,256]{1,0:T(8,128)(2,1)S(1)}, u32[]{:S(2)}, u32[]{:S(2)}) collective-permute-start(bf16[512,256]{1,0:T(8,128)(2,1)S(1)} %get-tuple-element.13), channel_id=1, source_target_pairs={{0,96},{32,128},{64,160},{96,192},{128,224},{1,97},{33,129},{65,16... | collective-permute-start | bytes 786440 | tf_op jit(solution)/shard_map/ppermute | solution.py:15
  83.4 3.5 copy-start.2
  343.1 12.3 %slice-start = ((s8[5242880]{0:T(1024)(128)(4,1)}), s8[4194304]{0:T(1024)(128)(4,1)S(1)}, s32[]{:S(2)}) async-start(s8[5242880]{0:T(1024)(128)(4,1)} %bitcast.104), calls=%async_computation.2 | async-start | bytes 8388608
  345.5 21.0 %collective-permute-start.3 = (bf16[512,256]{1,0:T(8,128)(2,1)S(1)}, bf16[512,256]{1,0:T(8,128)(2,1)S(1)}, u32[]{:S(2)}, u32[]{:S(2)}) collective-permute-start(bf16[512,256]{1,0:T(8,128)(2,1)S(1)} %fusion.57), channel_id=1, source_target_pairs={{32,0},{64,32},{96,64},{128,96},{160,128},{192,160},{224,192},{33,... | collective-permute-start | bytes 786440 | tf_op jit(solution)/shard_map/ppermute | solution.py:15
  350.5 4.9 %slice-start.1 = ((s8[5242880]{0:T(1024)(128)(4,1)}), s8[1048576]{0:T(1024)(128)(4,1)S(1)}, s32[]{:S(2)}) async-start(s8[5242880]{0:T(1024)(128)(4,1)} %bitcast.104), calls=%async_computation.3 | async-start | bytes 2097152
  352.8 13.7 %collective-permute-start.4 = (bf16[512,256]{1,0:T(8,128)(2,1)S(1)}, bf16[512,256]{1,0:T(8,128)(2,1)S(1)}, u32[]{:S(2)}, u32[]{:S(2)}) collective-permute-start(bf16[512,256]{1,0:T(8,128)(2,1)S(1)} %fusion.54), channel_id=1, source_target_pairs={{64,0},{96,32},{128,64},{160,96},{192,128},{224,160},{65,1},{97,33... | collective-permute-start | bytes 786440 | tf_op jit(solution)/shard_map/ppermute | solution.py:15
  356.3 10.8 %collective-permute-start.5 = (bf16[512,256]{1,0:T(8,128)(2,1)S(1)}, bf16[512,256]{1,0:T(8,128)(2,1)S(1)}, u32[]{:S(2)}, u32[]{:S(2)}) collective-permute-start(bf16[512,256]{1,0:T(8,128)(2,1)S(1)} %fusion.51), channel_id=1, source_target_pairs={{96,0},{128,32},{160,64},{192,96},{224,128},{97,1},{129,33},{161,6... | collective-permute-start | bytes 786440 | tf_op jit(solution)/shard_map/ppermute | solution.py:15
Sparse Core Ops, SparseCore 0:
  9.8 46.6 all-gather.1
  88.7 251.2 all-reduce.1
where the time goes:
time: 381 us; the launch traced here: 376 us
  waiting for transfers between devices  312 us (82%)
  matrix products  18.8 us (5%)
  starting transfers between devices  18.5 us (5%)
  between operations  14.3 us (4%)
  other arithmetic  11.5 us (3%)
    psum x1, waiting for transfers between devices, shards(): misfit = lax.psum(partial_value, ('latent', 'dp'))  248 us
    all_gather x1, waiting for transfers between devices, shards(): lax.all_gather(inputs, 'dp', axis=0, tiled=True)[:, 0]  48.5 us
    ppermute x6, starting transfers between devices, shifted_2(): return lax.ppermute(block, axis, route)  18.4 us
    ppermute x6, waiting for transfers between devices, shifted_2(): return lax.ppermute(block, axis, route)  15 us
  transfers between devices with their start and end apart: 8, of which 5 were waited for; matrix products, arithmetic and copies ran while one was open for 4% of the time, Pallas kernels for 0%

commit v1 on v0

v1 whole, which is shorter than its diff:
```python
import math

import jax
import jax.numpy as jnp
from jax import lax
from jax.sharding import PartitionSpec as P

SPARSITY = 1.0
EPSILON = 1e-06
Z = 8
CORES = 2


def over_layers(block, distance):
    count = lax.axis_size("layer")
    route = [(i - distance, i) for i in range(count) if 0 <= i - distance < count]
    return lax.ppermute(block, "layer", route)


def over_core(block):
    return lax.ppermute(block, "latent", [(i, i ^ 1) for i in range(Z * CORES)])


def over_dp(block):
    return lax.ppermute(block, "dp", [(0, 1), (1, 0)])


def over_z(block, distance):
    count = Z * CORES
    return lax.ppermute(
        block, "latent", [(i, (i + CORES * distance) % count) for i in range(count)]
    )


def to_owner(block):
    route = []
    for z in range(Z):
        for core in range(CORES):
            for dp in range(2):
                token_block = (1 - dp) * Z * CORES + core * Z + z
                route.append((token_block, (z * CORES + core) * 2 + dp))
    return lax.ppermute(block, ("latent", "dp"), route)


def rotated(rows, core, z):
    width = rows.shape[1]
    cut = rows.reshape(CORES, Z, -1, width)
    cut = jnp.where(core == 0, cut, cut[::-1])
    twice = jnp.concatenate([cut, cut], axis=1)
    return lax.dynamic_slice_in_dim(twice, z, Z, 1).reshape(rows.shape)


def restored(rows, core, z):
    width = rows.shape[1]
    cut = rows.reshape(CORES, Z, -1, width)
    cut = jnp.where(core == 0, cut, cut[::-1])
    twice = jnp.concatenate([cut, cut], axis=1)
    return lax.dynamic_slice_in_dim(twice, Z - z, Z, 1).reshape(rows.shape)


def shards(inputs, targets, w_enc, b_enc, w_dec):
    reach_count = w_dec.shape[1]
    latent = lax.axis_index("latent")
    z, core = latent // CORES, latent % CORES
    dp = lax.axis_index("dp")
    weights = w_dec[0]
    enc_weight = w_enc[0]
    half = inputs.shape[0]
    group = half // CORES
    piece = group // Z
    token_count = 2 * half
    loss_scale = 1.0 / math.sqrt(token_count)
    penalty = SPARSITY * loss_scale

    def encode(rows):
        preact = jnp.dot(rows, enc_weight, preferred_element_type=jnp.float32) + b_enc[0]
        return jnp.maximum(preact, 0.0).astype(jnp.bfloat16)

    def decode(sources):
        total = jnp.dot(sources[0], weights[0], preferred_element_type=jnp.float32)
        for k in range(1, reach_count):
            total = total + jnp.dot(sources[k], weights[k], preferred_element_type=jnp.float32)
        return total

    def spread(latents):
        return [latents] + [over_layers(latents, k) for k in range(1, reach_count)]

    own_x = rotated(inputs[:, 0], core, z)
    far_x0 = over_dp(own_x[:group])
    own_targets = to_owner(targets[:, 0])
    far_x1 = over_core(far_x0)

    near = spread(encode(own_x))
    near_sum = decode(near)
    near_part = near_sum[:group] + over_core(near_sum[group:])
    from_dp = over_dp(near_part.astype(jnp.bfloat16))

    far = spread(encode(jnp.concatenate([far_x0, far_x1], axis=0)))
    far_sum = decode(far)
    far_part = far_sum[:group] + over_core(far_sum[group:]) + from_dp.astype(jnp.float32)
    total = far_part[:piece]
    narrow = far_part.astype(jnp.bfloat16)
    for d in (4, 3, 5, 2, 6, 1, 7):
        total = total + over_z(narrow[d * piece : (d + 1) * piece], d).astype(jnp.float32)
    misfit = total - own_targets.astype(jnp.float32)
    grad_own = (misfit * loss_scale).astype(jnp.bfloat16)

    gathered = [grad_own] + [None] * (Z - 1)
    for d in (4, 3, 5, 2, 6, 1, 7):
        gathered[d] = over_z(grad_own, -d)
    far_g0 = jnp.concatenate(gathered, axis=0)
    near_g0 = over_dp(far_g0)
    far_g1 = over_core(far_g0)
    near_g1 = over_core(near_g0)
    far_g = jnp.concatenate([far_g0, far_g1], axis=0)
    near_g = jnp.concatenate([near_g0, near_g1], axis=0)

    column_norms = jnp.sqrt(jnp.sum(jnp.square(weights.astype(jnp.float32)), axis=2) + EPSILON)

    def back(grad):
        total = None
        for k in range(reach_count):
            term = lax.dot_general(
                grad, weights[k], (((1,), (1,)), ((), ())), preferred_element_type=jnp.float32
            )
            term = term + penalty * column_norms[k][None, :]
            if k == 0:
                total = term
            else:
                total = total + over_layers(term.astype(jnp.bfloat16), -k).astype(jnp.float32)
        return total

    far_up = back(far_g)
    near_up = back(near_g)
    pieces = []
    for k in range(reach_count):
        contrib = lax.dot_general(
            far[k], far_g, (((0,), (0,)), ((), ())), preferred_element_type=jnp.float32
        ) + lax.dot_general(
            near[k], near_g, (((0,), (0,)), ((), ())), preferred_element_type=jnp.float32
        )
        mass = jnp.sum(far[k].astype(jnp.float32), axis=0) + jnp.sum(
            near[k].astype(jnp.float32), axis=0
        )
        contrib = contrib + (penalty * mass / column_norms[k])[:, None] * weights[k].astype(
            jnp.float32
        )
        pieces.append(contrib.astype(jnp.bfloat16))
    grad_dec = jnp.stack(pieces)[None]
    far_up = restored(far_up, core, z)
    near_up = restored(near_up, core, z)
    upward = jnp.concatenate(
        [jnp.where(dp == 0, near_up, far_up), jnp.where(dp == 0, far_up, near_up)], axis=0
    )
    return (grad_dec, upward[:, None, :])


def solution(mesh):
    placed = (
        P("dp", "layer", None),
        P(("latent", "dp"), "layer", None),
        P("layer", None, ("latent", "dp")),
        P("layer", ("latent", "dp")),
        P("layer", None, ("latent", "dp"), None),
    )
    return jax.shard_map(
        shards,
        mesh=mesh,
        in_specs=placed,
        out_specs=(P("layer", None, ("latent", "dp"), None), P(None, "layer", ("latent", "dp"))),
        check_vma=False,
    )
```

time: 381 us -> 177 us (0.46); the launches traced: 376 us -> 177 us
  waiting for transfers between devices: 312 us -> 68.3 us
  starting transfers between devices: 18.5 us -> 78.9 us
  between operations: 14.3 us -> 1.36 us
    psum x1 -> x0, waiting for transfers between devices: 248 us -> none  [shards(): misfit = lax.psum(partial_value, ('latent', 'dp'))]
    ppermute x6 -> x35, starting transfers between devices: 18.4 us -> 78.9 us  [the longest x12 43.2 us: over_layers(): return lax.ppermute(block, 'layer', route)]
    ppermute x6 -> x35, waiting for transfers between devices: 15 us -> 68.3 us  [the longest x3 28.3 us: over_dp(): return lax.ppermute(block, 'dp', [(0, 1), (1, 0)])]
    all_gather x1 -> x0, waiting for transfers between devices: 48.5 us -> none  [shards(): lax.all_gather(inputs, 'dp', axis=0, tiled=True)[:, 0]]
    dot_general x13 -> x26, matrix products: 18.8 us -> 19.1 us  [the longest x6 6.67 us: decode(): jnp.dot(sources[k], weights[k], preferred_element_type=jnp.float32)]
  transfers between devices with their start and end apart: 8 -> 35, of which waited for: 5 -> 13; matrix products, arithmetic and copies ran while one was open for 4% -> 12% of each run, Pallas kernels for 0% -> 0%
where the time goes in v1:
time: 177 us
  starting transfers between devices  78.9 us (45%)
  waiting for transfers between devices  68.3 us (39%)
  matrix products  19.1 us (11%)
  other arithmetic  7.74 us (4%)
    ppermute x12, starting transfers between devices, over_layers(): return lax.ppermute(block, 'layer', route)  43.2 us
    ppermute x3, waiting for transfers between devices, over_dp(): return lax.ppermute(block, 'dp', [(0, 1), (1, 0)])  28.3 us
    ppermute x14, starting transfers between devices, over_z(): lax.ppermute(block, 'latent', [(i, (i + CORES * distance) % count) for i...  27.5 us
    ppermute x14, waiting for transfers between devices, over_z(): lax.ppermute(block, 'latent', [(i, (i + CORES * distance) % count) for i...  26.8 us
    ppermute x12, waiting for transfers between devices, over_layers(): return lax.ppermute(block, 'layer', route)  11.3 us
    dot_general x6, matrix products, decode(): jnp.dot(sources[k], weights[k], preferred_element_type=jnp.float32)  6.67 us
    ppermute x1, starting transfers between devices, to_owner(): return lax.ppermute(block, ('latent', 'dp'), route)  6.02 us
    dot_general x8, matrix products, back(): lax.dot_general(grad, weights[k], (((1,), (1,)), ((), ())), preferred_ele...  4.28 us
  transfers between devices with their start and end apart: 35, of which 13 were waited for; matrix products, arithmetic and copies ran while one was open for 12% of the time, Pallas kernels for 0%

profile of v1, /device:TPU:38, one launch (start us, length us, event | category | flops | bytes accessed | tf_op | source)
XLA Modules:
  0.0 177.0 jit_solution(4848551170116915882)
XLA Ops:
  0.7 2.2 %reverse_select_fusion = bf16[2,8,16,2560]{3,2,1,0:T(8,128)(2,1)S(1)} fusion(bf16[2,8,16,2560]{3,2,1,0:T(8,128)(2,1)} %bitcast.164, pred[]{:T(512)S(6)} %eq.6), kind=kLoop, calls=%fused_computation.26 | loop fusion | flops 655360 | bytes 2621441 | tf_op jit(solution)/shard_map/jit(_where)/select_n | solution.py:48
  6.7 5.1 %collective-permute-start.6 = (bf16[256,256]{1,0:T(8,128)(2,1)S(1)}, bf16[256,256]{1,0:T(8,128)(2,1)S(1)}, u32[]{:S(2)}, u32[]{:S(2)}) collective-permute-start(bf16[256,256]{1,0:T(8,128)(2,1)S(1)} %get-tuple-element.40), channel_id=1, source_target_pairs={{0,32},{32,64},{64,96},{96,128},{128,160},{160,192},{192,224},{1,3... | collective-permute-start | bytes 393224 | tf_op jit(solution)/shard_map/ppermute | solution.py:17
  11.8 6.0 %collective-permute-start.18 = (bf16[16,2560]{1,0:T(8,128)(2,1)S(1)}, bf16[16,2560]{1,0:T(8,128)(2,1)S(1)}, u32[]{:S(2)}, u32[]{:S(2)}) collective-permute-start(bf16[16,2560]{1,0:T(8,128)(2,1)S(1)} %bitcast.182), channel_id=1, source_target_pairs={{16,0},{0,1},{24,2},{8,3},{17,4},{1,5},{25,6},{9,7},{18,8},{2,9},{... | collective-permute-start | bytes 245768 | tf_op jit(solution)/shard_map/ppermute | solution.py:42
  22.2 2.8 %convolution_add_fusion.5 = f32[256,2560]{1,0:T(8,128)S(1)} fusion(f32[256,2560]{1,0:T(8,128)} %fusion.45, bf16[256,256]{1,0:T(8,128)(2,1)S(1)} %collective-permute-done.6, bf16[1,4,256,2560]{3,2,1,0:T(8,128)(2,1)} %param.9), kind=kOutput, calls=%fused_computation.7 | convolution fusion | flops 336199680 | bytes 6684672 | tf_op jit(solution)/shard_map/dot_general | solution.py:82
  25.0 10.2 %collective-permute-done = bf16[128,2560]{1,0:T(8,128)(2,1)S(1)} collective-permute-done((bf16[128,2560]{1,0:T(8,128)(2,1)S(1)}, bf16[128,2560]{1,0:T(8,128)(2,1)S(1)}, u32[]{:S(2)}, u32[]{:S(2)}) %collective-permute-start) | collective-permute-done | bytes 655392 | tf_op jit(solution)/shard_map/ppermute | solution.py:25
  41.4 2.7 %collective-permute-start.2 = (bf16[256,256]{1,0:T(8,128)(2,1)S(1)}, bf16[256,256]{1,0:T(8,128)(2,1)S(1)}, u32[]{:S(2)}, u32[]{:S(2)}) collective-permute-start(bf16[256,256]{1,0:T(8,128)(2,1)S(1)} %get-tuple-element.38), channel_id=1, source_target_pairs={{0,32},{32,64},{64,96},{96,128},{128,160},{160,192},{192,224},{1,3... | collective-permute-start | bytes 393224 | tf_op jit(solution)/shard_map/ppermute | solution.py:17
  44.6 10.3 %collective-permute-done.2 = bf16[256,256]{1,0:T(8,128)(2,1)S(1)} collective-permute-done((bf16[256,256]{1,0:T(8,128)(2,1)S(1)}, bf16[256,256]{1,0:T(8,128)(2,1)S(1)}, u32[]{:S(2)}, u32[]{:S(2)}) %collective-permute-start.2) | collective-permute-done | bytes 131104 | tf_op jit(solution)/shard_map/ppermute | solution.py:17
  57.1 16.9 %collective-permute-done.10 = bf16[128,2560]{1,0:T(8,128)(2,1)S(1)} collective-permute-done((bf16[128,2560]{1,0:T(8,128)(2,1)S(1)}, bf16[128,2560]{1,0:T(8,128)(2,1)S(1)}, u32[]{:S(2)}, u32[]{:S(2)}) %collective-permute-start.10) | collective-permute-done | bytes 655392 | tf_op jit(solution)/shard_map/ppermute | solution.py:25
  74.2 3.7 %collective-permute-start.11 = (bf16[16,2560]{1,0:T(8,128)(2,1)S(1)}, bf16[16,2560]{1,0:T(8,128)(2,1)S(1)}, u32[]{:S(2)}, u32[]{:S(2)}) collective-permute-start(bf16[16,2560]{1,0:T(8,128)(2,1)S(1)} %get-tuple-element.6), channel_id=1, source_target_pairs={{0,16},{2,18},{4,20},{6,22},{8,24},{10,26},{12,28},{14,30},{16,0},... | collective-permute-start | bytes 245768 | tf_op jit(solution)/shard_map/ppermute | solution.py:30
  80.1 2.1 %collective-permute-start.15 = (bf16[16,2560]{1,0:T(8,128)(2,1)S(1)}, bf16[16,2560]{1,0:T(8,128)(2,1)S(1)}, u32[]{:S(2)}, u32[]{:S(2)}) collective-permute-start(bf16[16,2560]{1,0:T(8,128)(2,1)S(1)} %get-tuple-element.9), channel_id=1, source_target_pairs={{0,24},{2,26},{4,28},{6,30},{8,0},{10,2},{12,4},{14,6},{16,8},{18,... | collective-permute-start | bytes 245768 | tf_op jit(solution)/shard_map/ppermute | solution.py:30
  89.9 5.2 %collective-permute-done.13 = bf16[16,2560]{1,0:T(8,128)(2,1)S(1)} collective-permute-done((bf16[16,2560]{1,0:T(8,128)(2,1)S(1)}, bf16[16,2560]{1,0:T(8,128)(2,1)S(1)}, u32[]{:S(2)}, u32[]{:S(2)}) %collective-permute-start.13) | collective-permute-done | bytes 81952 | tf_op jit(solution)/shard_map/ppermute | solution.py:30
  97.1 2.4 %collective-permute-start.24 = (bf16[16,2560]{1,0:T(8,128)(2,1)S(1)}, bf16[16,2560]{1,0:T(8,128)(2,1)S(1)}, u32[]{:S(2)}, u32[]{:S(2)}) collective-permute-start(bf16[16,2560]{1,0:T(8,128)(2,1)S(1)} %get-tuple-element.3), channel_id=1, source_target_pairs={{0,8},{2,10},{4,12},{6,14},{8,16},{10,18},{12,20},{14,22},{16,24},... | collective-permute-start | bytes 245768 | tf_op jit(solution)/shard_map/ppermute | solution.py:30
  100.1 3.4 %collective-permute-start.22 = (bf16[16,2560]{1,0:T(8,128)(2,1)S(1)}, bf16[16,2560]{1,0:T(8,128)(2,1)S(1)}, u32[]{:S(2)}, u32[]{:S(2)}) collective-permute-start(bf16[16,2560]{1,0:T(8,128)(2,1)S(1)} %get-tuple-element.3), channel_id=1, source_target_pairs={{0,16},{2,18},{4,20},{6,22},{8,24},{10,26},{12,28},{14,30},{16,0},... | collective-permute-start | bytes 245768 | tf_op jit(solution)/shard_map/ppermute | solution.py:30
  105.1 6.5 %collective-permute-done.19 = bf16[16,2560]{1,0:T(8,128)(2,1)S(1)} collective-permute-done((bf16[16,2560]{1,0:T(8,128)(2,1)S(1)}, bf16[16,2560]{1,0:T(8,128)(2,1)S(1)}, u32[]{:S(2)}, u32[]{:S(2)}) %collective-permute-start.19) | collective-permute-done | bytes 81952 | tf_op jit(solution)/shard_map/ppermute | solution.py:30
  111.6 3.4 %collective-permute-start.20 = (bf16[16,2560]{1,0:T(8,128)(2,1)S(1)}, bf16[16,2560]{1,0:T(8,128)(2,1)S(1)}, u32[]{:S(2)}, u32[]{:S(2)}) collective-permute-start(bf16[16,2560]{1,0:T(8,128)(2,1)S(1)} %get-tuple-element.3), channel_id=1, source_target_pairs={{0,24},{2,26},{4,28},{6,30},{8,0},{10,2},{12,4},{14,6},{16,8},{18,... | collective-permute-start | bytes 245768 | tf_op jit(solution)/shard_map/ppermute | solution.py:30
  115.0 4.6 %collective-permute-done.20 = bf16[16,2560]{1,0:T(8,128)(2,1)S(1)} collective-permute-done((bf16[16,2560]{1,0:T(8,128)(2,1)S(1)}, bf16[16,2560]{1,0:T(8,128)(2,1)S(1)}, u32[]{:S(2)}, u32[]{:S(2)}) %collective-permute-start.20) | collective-permute-done | bytes 81952 | tf_op jit(solution)/shard_map/ppermute | solution.py:30
  119.6 3.6 %collective-permute-start.21 = (bf16[16,2560]{1,0:T(8,128)(2,1)S(1)}, bf16[16,2560]{1,0:T(8,128)(2,1)S(1)}, u32[]{:S(2)}, u32[]{:S(2)}) collective-permute-start(bf16[16,2560]{1,0:T(8,128)(2,1)S(1)} %get-tuple-element.3), channel_id=1, source_target_pairs={{0,20},{2,22},{4,24},{6,26},{8,28},{10,30},{12,0},{14,2},{16,4},{1... | collective-permute-start | bytes 245768 | tf_op jit(solution)/shard_map/ppermute | solution.py:30
  123.2 5.6 %collective-permute-done.21 = bf16[16,2560]{1,0:T(8,128)(2,1)S(1)} collective-permute-done((bf16[16,2560]{1,0:T(8,128)(2,1)S(1)}, bf16[16,2560]{1,0:T(8,128)(2,1)S(1)}, u32[]{:S(2)}, u32[]{:S(2)}) %collective-permute-start.21) | collective-permute-done | bytes 81952 | tf_op jit(solution)/shard_map/ppermute | solution.py:30
  134.2 5.7 %collective-permute-start.33 = (bf16[256,256]{1,0:T(8,128)(2,1)S(1)}, bf16[256,256]{1,0:T(8,128)(2,1)S(1)}, u32[]{:S(2)}, u32[]{:S(2)}) collective-permute-start(bf16[256,256]{1,0:T(8,128)(2,1)S(1)} %fusion.116), channel_id=1, source_target_pairs={{64,0},{96,32},{128,64},{160,96},{192,128},{224,160},{65,1},{97,33... | collective-permute-start | bytes 393224 | tf_op jit(solution)/shard_map/ppermute | solution.py:17
  140.4 4.7 %collective-permute-start.34 = (bf16[256,256]{1,0:T(8,128)(2,1)S(1)}, bf16[256,256]{1,0:T(8,128)(2,1)S(1)}, u32[]{:S(2)}, u32[]{:S(2)}) collective-permute-start(bf16[256,256]{1,0:T(8,128)(2,1)S(1)} %fusion.110), channel_id=1, source_target_pairs={{96,0},{128,32},{160,64},{192,96},{224,128},{97,1},{129,33},{161,6... | collective-permute-start | bytes 393224 | tf_op jit(solution)/shard_map/ppermute | solution.py:17
  150.1 5.0 %collective-permute-start.29 = (bf16[256,256]{1,0:T(8,128)(2,1)S(1)}, bf16[256,256]{1,0:T(8,128)(2,1)S(1)}, u32[]{:S(2)}, u32[]{:S(2)}) collective-permute-start(bf16[256,256]{1,0:T(8,128)(2,1)S(1)} %fusion.125), channel_id=1, source_target_pairs={{32,0},{64,32},{96,64},{128,96},{160,128},{192,160},{224,192},{33,... | collective-permute-start | bytes 393224 | tf_op jit(solution)/shard_map/ppermute | solution.py:17
  155.1 5.3 %collective-permute-start.30 = (bf16[256,256]{1,0:T(8,128)(2,1)S(1)}, bf16[256,256]{1,0:T(8,128)(2,1)S(1)}, u32[]{:S(2)}, u32[]{:S(2)}) collective-permute-start(bf16[256,256]{1,0:T(8,128)(2,1)S(1)} %fusion.119), channel_id=1, source_target_pairs={{64,0},{96,32},{128,64},{160,96},{192,128},{224,160},{65,1},{97,33... | collective-permute-start | bytes 393224 | tf_op jit(solution)/shard_map/ppermute | solution.py:17
  160.5 7.5 %collective-permute-start.31 = (bf16[256,256]{1,0:T(8,128)(2,1)S(1)}, bf16[256,256]{1,0:T(8,128)(2,1)S(1)}, u32[]{:S(2)}, u32[]{:S(2)}) collective-permute-start(bf16[256,256]{1,0:T(8,128)(2,1)S(1)} %fusion.113), channel_id=1, source_target_pairs={{96,0},{128,32},{160,64},{192,96},{224,128},{97,1},{129,33},{161,6... | collective-permute-start | bytes 393224 | tf_op jit(solution)/shard_map/ppermute | solution.py:17
  172.1 2.9 %maximum_bitcast_fusion = bf16[1,4,256,2560]{3,2,1,0:T(8,128)(2,1)} fusion(bf16[1,256,2560]{2,1,0:T(8,128)(2,1)S(1)} %fusion.13, bf16[1,256,2560]{2,1,0:T(8,128)(2,1)S(1)} %fusion.12, bf16[1,256,2560]{2,1,0:T(8,128)(2,1)S(1)} %fusion.11, bf16[1,256,2560]{2,1,0:T(8,128)(2,1)S(1)} %fusion.10), kind=kLoop, calls=%fused_computation.1 | loop fusion | flops 7864320 | bytes 10485760 | tf_op jit(solution)/shard_map/broadcast_in_dim | solution.py:149
  (125 shorter events, 47.8 us)
Async XLA Ops:
  4.0 31.2 %collective-permute-start.8 = (bf16[256,256]{1,0:T(8,128)(2,1)S(1)}, bf16[256,256]{1,0:T(8,128)(2,1)S(1)}, u32[]{:S(2)}, u32[]{:S(2)}) collective-permute-start(bf16[256,256]{1,0:T(8,128)(2,1)S(1)} %get-tuple-element.40), channel_id=1, source_target_pairs={{0,96},{32,128},{64,160},{96,192},{128,224},{1,97},{33,129},{65,16... | collective-permute-start | bytes 393224 | tf_op jit(solution)/shard_map/ppermute | solution.py:17
  5.4 31.6 %collective-permute-start.7 = (bf16[256,256]{1,0:T(8,128)(2,1)S(1)}, bf16[256,256]{1,0:T(8,128)(2,1)S(1)}, u32[]{:S(2)}, u32[]{:S(2)}) collective-permute-start(bf16[256,256]{1,0:T(8,128)(2,1)S(1)} %get-tuple-element.40), channel_id=1, source_target_pairs={{0,64},{32,96},{64,128},{96,160},{128,192},{160,224},{1,65},{33,97... | collective-permute-start | bytes 393224 | tf_op jit(solution)/shard_map/ppermute | solution.py:17
  6.7 15.4 %collective-permute-start.6 = (bf16[256,256]{1,0:T(8,128)(2,1)S(1)}, bf16[256,256]{1,0:T(8,128)(2,1)S(1)}, u32[]{:S(2)}, u32[]{:S(2)}) collective-permute-start(bf16[256,256]{1,0:T(8,128)(2,1)S(1)} %get-tuple-element.40), channel_id=1, source_target_pairs={{0,32},{32,64},{64,96},{96,128},{128,160},{160,192},{192,224},{1,3... | collective-permute-start | bytes 393224 | tf_op jit(solution)/shard_map/ppermute | solution.py:17
  11.8 70.4 %collective-permute-start.18 = (bf16[16,2560]{1,0:T(8,128)(2,1)S(1)}, bf16[16,2560]{1,0:T(8,128)(2,1)S(1)}, u32[]{:S(2)}, u32[]{:S(2)}) collective-permute-start(bf16[16,2560]{1,0:T(8,128)(2,1)S(1)} %bitcast.182), channel_id=1, source_target_pairs={{16,0},{0,1},{24,2},{8,3},{17,4},{1,5},{25,6},{9,7},{18,8},{2,9},{... | collective-permute-start | bytes 245768 | tf_op jit(solution)/shard_map/ppermute | solution.py:42
  17.9 17.3 %collective-permute-start = (bf16[128,2560]{1,0:T(8,128)(2,1)S(1)}, bf16[128,2560]{1,0:T(8,128)(2,1)S(1)}, u32[]{:S(2)}, u32[]{:S(2)}) collective-permute-start(bf16[128,2560]{1,0:T(8,128)(2,1)S(1)} %bitcast.167), channel_id=1, source_target_pairs={{0,1},{1,0},{2,3},{3,2},{4,5},{5,4},{6,7},{7,6},{8,9},{9,8},{10,11... | collective-permute-start | bytes 1966088 | tf_op jit(solution)/shard_map/ppermute | solution.py:25
  37.7 18.9 %collective-permute-start.9 = (f32[128,2560]{1,0:T(8,128)S(1)}, f32[128,2560]{1,0:T(8,128)S(1)}, u32[]{:S(2)}, u32[]{:S(2)}) collective-permute-start(f32[128,2560]{1,0:T(8,128)S(1)} %slice.120), channel_id=1, source_target_pairs={{0,2},{2,0},{4,6},{6,4},{8,10},{10,8},{12,14},{14,12},{16,18},{18,... | collective-permute-start | bytes 3932168 | tf_op jit(solution)/shard_map/ppermute | solution.py:21
  38.8 16.6 %collective-permute-start.4 = (bf16[256,256]{1,0:T(8,128)(2,1)S(1)}, bf16[256,256]{1,0:T(8,128)(2,1)S(1)}, u32[]{:S(2)}, u32[]{:S(2)}) collective-permute-start(bf16[256,256]{1,0:T(8,128)(2,1)S(1)} %get-tuple-element.38), channel_id=1, source_target_pairs={{0,96},{32,128},{64,160},{96,192},{128,224},{1,97},{33,129},{65,16... | collective-permute-start | bytes 393224 | tf_op jit(solution)/shard_map/ppermute | solution.py:17
  40.1 15.8 %collective-permute-start.3 = (bf16[256,256]{1,0:T(8,128)(2,1)S(1)}, bf16[256,256]{1,0:T(8,128)(2,1)S(1)}, u32[]{:S(2)}, u32[]{:S(2)}) collective-permute-start(bf16[256,256]{1,0:T(8,128)(2,1)S(1)} %get-tuple-element.38), channel_id=1, source_target_pairs={{0,64},{32,96},{64,128},{96,160},{128,192},{160,224},{1,65},{33,97... | collective-permute-start | bytes 393224 | tf_op jit(solution)/shard_map/ppermute | solution.py:17
  41.4 13.4 %collective-permute-start.2 = (bf16[256,256]{1,0:T(8,128)(2,1)S(1)}, bf16[256,256]{1,0:T(8,128)(2,1)S(1)}, u32[]{:S(2)}, u32[]{:S(2)}) collective-permute-start(bf16[256,256]{1,0:T(8,128)(2,1)S(1)} %get-tuple-element.38), channel_id=1, source_target_pairs={{0,32},{32,64},{64,96},{96,128},{128,160},{160,192},{192,224},{1,3... | collective-permute-start | bytes 393224 | tf_op jit(solution)/shard_map/ppermute | solution.py:17
  56.5 17.5 %collective-permute-start.5 = (f32[128,2560]{1,0:T(8,128)S(1)}, f32[128,2560]{1,0:T(8,128)S(1)}, u32[]{:S(2)}, u32[]{:S(2)}) collective-permute-start(f32[128,2560]{1,0:T(8,128)S(1)} %slice.118), channel_id=1, source_target_pairs={{0,2},{2,0},{4,6},{6,4},{8,10},{10,8},{12,14},{14,12},{16,18},{18,... | collective-permute-start | bytes 3932168 | tf_op jit(solution)/shard_map/ppermute | solution.py:21
  56.8 17.2 %collective-permute-start.10 = (bf16[128,2560]{1,0:T(8,128)(2,1)S(1)}, bf16[128,2560]{1,0:T(8,128)(2,1)S(1)}, u32[]{:S(2)}, u32[]{:S(2)}) collective-permute-start(bf16[128,2560]{1,0:T(8,128)(2,1)S(1)} %fusion.15), channel_id=1, source_target_pairs={{0,1},{1,0},{2,3},{3,2},{4,5},{5,4},{6,7},{7,6},{8,9},{9,8},{10,11... | collective-permute-start | bytes 1966088 | tf_op jit(solution)/shard_map/ppermute | solution.py:25
  74.2 10.6 %collective-permute-start.11 = (bf16[16,2560]{1,0:T(8,128)(2,1)S(1)}, bf16[16,2560]{1,0:T(8,128)(2,1)S(1)}, u32[]{:S(2)}, u32[]{:S(2)}) collective-permute-start(bf16[16,2560]{1,0:T(8,128)(2,1)S(1)} %get-tuple-element.6), channel_id=1, source_target_pairs={{0,16},{2,18},{4,20},{6,22},{8,24},{10,26},{12,28},{14,30},{16,0},... | collective-permute-start | bytes 245768 | tf_op jit(solution)/shard_map/ppermute | solution.py:30
  78.0 11.9 %collective-permute-start.16 = (bf16[16,2560]{1,0:T(8,128)(2,1)S(1)}, bf16[16,2560]{1,0:T(8,128)(2,1)S(1)}, u32[]{:S(2)}, u32[]{:S(2)}) collective-permute-start(bf16[16,2560]{1,0:T(8,128)(2,1)S(1)} %get-tuple-element.8), channel_id=1, source_target_pairs={{0,4},{2,6},{4,8},{6,10},{8,12},{10,14},{12,16},{14,18},{16,20},{1... | collective-permute-start | bytes 245768 | tf_op jit(solution)/shard_map/ppermute | solution.py:30
  84.8 10.3 %collective-permute-start.13 = (bf16[16,2560]{1,0:T(8,128)(2,1)S(1)}, bf16[16,2560]{1,0:T(8,128)(2,1)S(1)}, u32[]{:S(2)}, u32[]{:S(2)}) collective-permute-start(bf16[16,2560]{1,0:T(8,128)(2,1)S(1)} %get-tuple-element.11), channel_id=1, source_target_pairs={{0,20},{2,22},{4,24},{6,26},{8,28},{10,30},{12,0},{14,2},{16,4},{1... | collective-permute-start | bytes 245768 | tf_op jit(solution)/shard_map/ppermute | solution.py:30
  97.0 31.9 %collective-permute-start.25 = (bf16[16,2560]{1,0:T(8,128)(2,1)S(1)}, bf16[16,2560]{1,0:T(8,128)(2,1)S(1)}, u32[]{:S(2)}, u32[]{:S(2)}) collective-permute-start(bf16[16,2560]{1,0:T(8,128)(2,1)S(1)} %get-tuple-element.3), channel_id=1, source_target_pairs={{0,4},{2,6},{4,8},{6,10},{8,12},{10,14},{12,16},{14,18},{16,20},{1... | collective-permute-start | bytes 245768 | tf_op jit(solution)/shard_map/ppermute | solution.py:30
  97.1 31.8 %collective-permute-start.24 = (bf16[16,2560]{1,0:T(8,128)(2,1)S(1)}, bf16[16,2560]{1,0:T(8,128)(2,1)S(1)}, u32[]{:S(2)}, u32[]{:S(2)}) collective-permute-start(bf16[16,2560]{1,0:T(8,128)(2,1)S(1)} %get-tuple-element.3), channel_id=1, source_target_pairs={{0,8},{2,10},{4,12},{6,14},{8,16},{10,18},{12,20},{14,22},{16,24},... | collective-permute-start | bytes 245768 | tf_op jit(solution)/shard_map/ppermute | solution.py:30
  99.4 29.4 %collective-permute-start.23 = (bf16[16,2560]{1,0:T(8,128)(2,1)S(1)}, bf16[16,2560]{1,0:T(8,128)(2,1)S(1)}, u32[]{:S(2)}, u32[]{:S(2)}) collective-permute-start(bf16[16,2560]{1,0:T(8,128)(2,1)S(1)} %get-tuple-element.3), channel_id=1, source_target_pairs={{0,12},{2,14},{4,16},{6,18},{8,20},{10,22},{12,24},{14,26},{16,28}... | collective-permute-start | bytes 245768 | tf_op jit(solution)/shard_map/ppermute | solution.py:30
  100.1 28.7 %collective-permute-start.22 = (bf16[16,2560]{1,0:T(8,128)(2,1)S(1)}, bf16[16,2560]{1,0:T(8,128)(2,1)S(1)}, u32[]{:S(2)}, u32[]{:S(2)}) collective-permute-start(bf16[16,2560]{1,0:T(8,128)(2,1)S(1)} %get-tuple-element.3), channel_id=1, source_target_pairs={{0,16},{2,18},{4,20},{6,22},{8,24},{10,26},{12,28},{14,30},{16,0},... | collective-permute-start | bytes 245768 | tf_op jit(solution)/shard_map/ppermute | solution.py:30
  129.1 17.2 %collective-permute-start.27 = (bf16[128,2560]{1,0:T(8,128)(2,1)S(1)}, bf16[128,2560]{1,0:T(8,128)(2,1)S(1)}, u32[]{:S(2)}, u32[]{:S(2)}) collective-permute-start(bf16[128,2560]{1,0:T(8,128)(2,1)S(1)} %get-tuple-element.16), channel_id=1, source_target_pairs={{0,1},{1,0},{2,3},{3,2},{4,5},{5,4},{6,7},{7,6},{8,9},{9,8},{10,11... | collective-permute-start | bytes 1966088 | tf_op jit(solution)/shard_map/ppermute | solution.py:25
  131.7 15.2 %collective-permute-start.32 = (bf16[256,256]{1,0:T(8,128)(2,1)S(1)}, bf16[256,256]{1,0:T(8,128)(2,1)S(1)}, u32[]{:S(2)}, u32[]{:S(2)}) collective-permute-start(bf16[256,256]{1,0:T(8,128)(2,1)S(1)} %fusion.122), channel_id=1, source_target_pairs={{32,0},{64,32},{96,64},{128,96},{160,128},{192,160},{224,192},{33,... | collective-permute-start | bytes 393224 | tf_op jit(solution)/shard_map/ppermute | solution.py:17
  134.2 12.7 %collective-permute-start.33 = (bf16[256,256]{1,0:T(8,128)(2,1)S(1)}, bf16[256,256]{1,0:T(8,128)(2,1)S(1)}, u32[]{:S(2)}, u32[]{:S(2)}) collective-permute-start(bf16[256,256]{1,0:T(8,128)(2,1)S(1)} %fusion.116), channel_id=1, source_target_pairs={{64,0},{96,32},{128,64},{160,96},{192,128},{224,160},{65,1},{97,33... | collective-permute-start | bytes 393224 | tf_op jit(solution)/shard_map/ppermute | solution.py:17
  150.1 24.9 %collective-permute-start.29 = (bf16[256,256]{1,0:T(8,128)(2,1)S(1)}, bf16[256,256]{1,0:T(8,128)(2,1)S(1)}, u32[]{:S(2)}, u32[]{:S(2)}) collective-permute-start(bf16[256,256]{1,0:T(8,128)(2,1)S(1)} %fusion.125), channel_id=1, source_target_pairs={{32,0},{64,32},{96,64},{128,96},{160,128},{192,160},{224,192},{33,... | collective-permute-start | bytes 393224 | tf_op jit(solution)/shard_map/ppermute | solution.py:17
  155.1 19.9 %collective-permute-start.30 = (bf16[256,256]{1,0:T(8,128)(2,1)S(1)}, bf16[256,256]{1,0:T(8,128)(2,1)S(1)}, u32[]{:S(2)}, u32[]{:S(2)}) collective-permute-start(bf16[256,256]{1,0:T(8,128)(2,1)S(1)} %fusion.119), channel_id=1, source_target_pairs={{64,0},{96,32},{128,64},{160,96},{192,128},{224,160},{65,1},{97,33... | collective-permute-start | bytes 393224 | tf_op jit(solution)/shard_map/ppermute | solution.py:17
  160.5 14.5 %collective-permute-start.31 = (bf16[256,256]{1,0:T(8,128)(2,1)S(1)}, bf16[256,256]{1,0:T(8,128)(2,1)S(1)}, u32[]{:S(2)}, u32[]{:S(2)}) collective-permute-start(bf16[256,256]{1,0:T(8,128)(2,1)S(1)} %fusion.113), channel_id=1, source_target_pairs={{96,0},{128,32},{160,64},{192,96},{224,128},{97,1},{129,33},{161,6... | collective-permute-start | bytes 393224 | tf_op jit(solution)/shard_map/ppermute | solution.py:17
  (18 other events, 137.8 us)

commit v2 on v1

v2 whole, which is shorter than its diff:
```python
import math

import jax
import jax.numpy as jnp
from jax import lax
from jax.sharding import PartitionSpec as P

SPARSITY = 1.0
EPSILON = 1e-06
Z = 8
CORES = 2
F32 = jnp.float32
BF16 = jnp.bfloat16


def over_layers(block, distance):
    count = lax.axis_size("layer")
    route = [(i - distance, i) for i in range(count) if 0 <= i - distance < count]
    return lax.ppermute(block, "layer", route)


def over_core(block):
    return lax.ppermute(block, "latent", [(i, i ^ 1) for i in range(Z * CORES)])


def over_dp(block):
    return lax.ppermute(block, "dp", [(0, 1), (1, 0)])


def over_z(block, distance):
    route = []
    for z in range(Z):
        route.append((z * CORES, (z + distance) % Z * CORES))
        route.append((z * CORES + 1, (z - distance) % Z * CORES + 1))
    return lax.ppermute(block, "latent", route)


def block_order(core, z):
    def served(own):
        step = 1 - 2 * own
        places = [2 * z + own]
        for k in (2, 3, 1):
            chunk = (z + step * k) % Z
            places += [2 * chunk + own, 2 * chunk + 1 - own]
        places.append(2 * ((z + Z // 2) % Z) + own)
        return places

    return jnp.stack(served(core) + served(1 - core))


def after(value, *others):
    return lax.optimization_barrier((value, *others))[0]


def shards(inputs, targets, w_enc, b_enc, w_dec):
    reach_count, width, channels = w_dec.shape[1:]
    latent = lax.axis_index("latent")
    z, core = latent // CORES, latent % CORES
    dp = lax.axis_index("dp")
    weights = w_dec[0]
    enc_weight = w_enc[0]
    half = inputs.shape[0]
    group = half // CORES
    piece = group // Z
    loss_scale = 1.0 / math.sqrt(2 * half)
    penalty = SPARSITY * loss_scale

    x = inputs[:, 0]
    far_x0 = over_dp(lax.dynamic_slice_in_dim(x, core * group, group, 0))

    order = block_order(core, z)
    token = (order[:, None] * piece + jnp.arange(piece)[None, :]).reshape(half)
    shuffle = (token[:, None] == jnp.arange(half)[None, :]).astype(BF16)
    swapped = jnp.where(core == 0, shuffle, jnp.roll(shuffle, group, axis=1))
    own_row = token[:, None] - (2 * latent + dp) % (2 * Z) * piece == jnp.arange(piece)[None, :]
    is_near = latent // Z == dp
    near_mark = (own_row & is_near).astype(BF16)
    far_mark = (own_row & ~is_near).astype(BF16)
    own_targets = targets[:, 0]

    def encode(rows, place):
        preact = jnp.dot(rows, enc_weight, preferred_element_type=F32) + b_enc[0]
        natural = jnp.maximum(preact, 0.0).astype(BF16)
        return jnp.dot(place, natural, preferred_element_type=F32).astype(BF16)

    def decode_first(source, mark):
        own = jnp.dot(mark, own_targets, preferred_element_type=F32)
        return jnp.dot(source, weights[0], preferred_element_type=F32) - own

    def decode_rest(total, sources):
        for k in range(1, reach_count):
            total, source = lax.optimization_barrier((total, sources[k]))
            total = total + jnp.dot(source, weights[k], preferred_element_type=F32)
        return total

    def spread(latents):
        return [latents] + [over_layers(latents, k) for k in range(1, reach_count)]

    cut = 3 * piece
    near = spread(encode(x, shuffle))
    near[0], near_mark, far_x0 = lax.optimization_barrier((near[0], near_mark, far_x0))
    near_sum = decode_first(near[0], near_mark)
    far_x1 = over_core(after(far_x0, near_sum))
    near_sum = decode_rest(near_sum, near)
    near_part = near_sum[:group] + over_core(near_sum[group:].astype(BF16)).astype(F32)
    near_part = near_part.astype(BF16)
    from_dp1 = over_dp(near_part[cut:])
    from_dp2 = over_dp(near_part[:cut])

    far_x1 = after(far_x1, near_sum)
    far = spread(encode(jnp.concatenate([far_x0, far_x1], axis=0), swapped))
    *far, from_dp1 = lax.optimization_barrier((*far, from_dp1))
    far_sum = decode_rest(decode_first(far[0], far_mark), far)
    part = far_sum[:group] + over_core(far_sum[group:].astype(BF16)).astype(F32)
    away = (part[cut:] + from_dp1.astype(F32)).astype(BF16)
    by_one = over_z(away[: 4 * piece], 1)
    by_two = over_z(away[4 * piece :], 2)
    by_one, by_two, from_dp2 = lax.optimization_barrier((by_one, by_two, from_dp2))
    home = part[:cut] + from_dp2.astype(F32)
    passing = home[piece:] + by_one[: 2 * piece].astype(F32)
    passing = jnp.concatenate([passing[:piece] + by_two.astype(F32), passing[piece:]], axis=0)
    got = over_z(passing.astype(BF16), 2).astype(F32) + by_one[2 * piece :].astype(F32)
    got = jnp.concatenate([got[:piece] + home[:piece], got[piece:]], axis=0)
    other = over_core(got)
    misfit = got + jnp.concatenate([other[piece:], other[:piece]], axis=0)
    pair = (misfit * loss_scale).astype(BF16)

    later_weights, pair = lax.optimization_barrier((weights, pair))
    norms = jnp.sqrt(jnp.sum(jnp.square(later_weights.astype(F32)), axis=2) + EPSILON)
    scales = []
    for k in range(reach_count):
        mass = jnp.sum(near[k].astype(F32), axis=0) + jnp.sum(far[k].astype(F32), axis=0)
        scales.append(penalty * mass / norms[k])

    g2 = over_z(pair, -2)
    g2, norms, scales = lax.optimization_barrier((g2, norms, scales))
    early = jnp.concatenate([pair[:piece], g2], axis=0)
    near_early = over_dp(early)
    g31 = over_z(jnp.concatenate([g2, pair], axis=0), -1)
    g4 = over_z(g2[:piece], -2)
    g31, g4, near_early = lax.optimization_barrier((g31, g4, near_early))
    late = jnp.concatenate([g31, g4], axis=0)
    near_late = over_dp(late)
    far_g0 = jnp.concatenate([early, late], axis=0)
    far_g1 = over_core(far_g0)

    def back(g0, g1):
        grad = lax.dot_general(
            shuffle,
            jnp.concatenate([g0, g1], axis=0),
            (((0,), (0,)), ((), ())),
            preferred_element_type=F32,
        ).astype(BF16)
        terms = []
        for k in range(reach_count):
            term = lax.dot_general(
                grad, weights[k], (((1,), (1,)), ((), ())), preferred_element_type=F32
            )
            terms.append(term + penalty * norms[k][None, :])
        return terms

    far_terms = back(far_g0, far_g1)
    far_two = jnp.concatenate([term.astype(BF16) for term in far_terms[2:]], axis=0)
    far_down = over_layers(far_two, -2).astype(F32)
    far_step = (far_terms[1] + far_down[half:]).astype(BF16)
    far_g = jnp.concatenate([far_g0, far_g1], axis=0)
    near_early, near_late = lax.optimization_barrier((near_early, near_late, far_terms))[:2]
    near_g0 = jnp.concatenate([near_early, near_late], axis=0)
    near_g1 = over_core(near_g0)
    near_g = jnp.concatenate([near_g0, near_g1], axis=0)
    near_terms = back(near_g0, near_g1)
    near_down3 = over_layers(near_terms[3].astype(BF16), -3).astype(F32)
    step = over_layers(jnp.concatenate([near_terms[1].astype(BF16), far_step], axis=0), -1)
    near_down2 = over_layers(near_terms[2].astype(BF16), -2).astype(F32)
    near_up = near_terms[0] + step[:half].astype(F32) + near_down2 + near_down3
    far_up = far_terms[0] + step[half:].astype(F32) + far_down[:half]
    upward = jnp.concatenate([far_up, near_up], axis=0)
    pieces = []
    for k in range(reach_count):
        contrib = lax.dot_general(
            far[k], far_g, (((0,), (0,)), ((), ())), preferred_element_type=F32
        ) + lax.dot_general(
            near[k], near_g, (((0,), (0,)), ((), ())), preferred_element_type=F32
        )
        contrib = contrib + scales[k][:, None] * weights[k].astype(F32)
        pieces.append(contrib.astype(BF16))
    grad_dec = jnp.stack(pieces)[None]
    out = jnp.concatenate([upward, upward[:half]], axis=0)
    out = lax.dynamic_slice_in_dim(out, (1 - dp) * half, 2 * half, 0)[:, None, :]
    return (grad_dec, out)


def solution(mesh):
    placed = (
        P("dp", "layer", None),
        P(("latent", "dp"), "layer", None),
        P("layer", None, ("latent", "dp")),
        P("layer", ("latent", "dp")),
        P("layer", None, ("latent", "dp"), None),
    )
    return jax.shard_map(
        shards,
        mesh=mesh,
        in_specs=placed,
        out_specs=(P("layer", None, ("latent", "dp"), None), P(None, "layer", ("latent", "dp"))),
        check_vma=False,
    )
```

time: 177 us -> 152 us (0.86); the launches traced: 177 us -> 149 us
  starting transfers between devices: 78.9 us -> 57.8 us
  waiting for transfers between devices: 68.3 us -> 48.5 us
  matrix products: 19.1 us -> 23.7 us
  local copies, waits for them, and re-layouts: 1.68 us -> 6.26 us
  other arithmetic: 7.74 us -> 10.8 us
    ppermute x15 -> x6, starting transfers between devices: 33.5 us -> 17.3 us  [over_z(): return lax.ppermute(block, 'latent', route)]
    ppermute x15 -> x6, waiting for transfers between devices: 26.8 us -> 13 us  [over_z(): return lax.ppermute(block, 'latent', route)]
    ppermute x3 -> x5, waiting for transfers between devices: 28.3 us -> 15.2 us  [over_dp(): return lax.ppermute(block, 'dp', [(0, 1), (1, 0)])]
    ppermute x12 -> x10, starting transfers between devices: 43.2 us -> 35.3 us  [over_layers(): return lax.ppermute(block, 'layer', route)]
    ppermute x5 -> x6, waiting for transfers between devices: 1.95 us -> 9.13 us  [over_core(): return lax.ppermute(block, 'latent', [(i, i ^ 1) for i in range(Z * CORES)])]
    dot_general x10 -> x14, matrix products: 10.2 us -> 14.8 us  [the longest x2 4.58 us: encode(): return jnp.dot(place, natural, preferred_element_type=F32).astype(BF16)]
    add x0 -> x10, other arithmetic: none -> 3.14 us  [the longest x1 0.95 us: shards(): passing = home[piece:] + by_one[:2 * piece].astype(F32)]
    unnamed x23 -> x66, local copies, waits for them, and re-layouts: 0.19 us -> 3.12 us
  transfers between devices with their start and end apart: 35 -> 27, of which waited for: 13 -> 16; matrix products, arithmetic and copies ran while one was open for 12% -> 16% of each run, Pallas kernels for 0% -> 0%
where the time goes in v2:
time: 152 us; the launch traced here: 149 us
  starting transfers between devices  57.8 us (38%)
  waiting for transfers between devices  48.5 us (32%)
  matrix products  23.7 us (16%)
  other arithmetic  10.8 us (7%)
  local copies, waits for them, and re-layouts  6.26 us (4%)
  between operations  1.7 us (1%)
    ppermute x10, starting transfers between devices, over_layers(): return lax.ppermute(block, 'layer', route)  35.3 us
    ppermute x6, starting transfers between devices, over_z(): return lax.ppermute(block, 'latent', route)  17.3 us
    ppermute x5, waiting for transfers between devices, over_dp(): return lax.ppermute(block, 'dp', [(0, 1), (1, 0)])  15.2 us
    ppermute x6, waiting for transfers between devices, over_z(): return lax.ppermute(block, 'latent', route)  13 us
    ppermute x10, waiting for transfers between devices, over_layers(): return lax.ppermute(block, 'layer', route)  11.2 us
    ppermute x6, waiting for transfers between devices, over_core(): return lax.ppermute(block, 'latent', [(i, i ^ 1) for i in range(Z * CORES)])  9.13 us
    dot_general x2, matrix products, encode(): return jnp.dot(place, natural, preferred_element_type=F32).astype(BF16)  4.58 us
    dot_general x8, matrix products, back(): lax.dot_general(grad, weights[k], (((1,), (1,)), ((), ())), preferred_ele...  4.32 us
  transfers between devices with their start and end apart: 27, of which 16 were waited for; matrix products, arithmetic and copies ran while one was open for 16% of the time, Pallas kernels for 0%

profile of v2, /device:TPU:38, one launch (start us, length us, event | category | flops | bytes accessed | tf_op | source)
XLA Modules:
  0.0 148.8 jit_solution(3415153887684568047)
XLA Ops:
  3.9 2.0 %convolution_convert_fusion.3 = bf16[256,256]{1,0:T(8,128)(2,1)S(1)} fusion(bf16[1,2560,256]{2,1,0:T(8,128)(2,1)} %param.7, bf16[256,1,2560]{2,0,1:T(8,128)(2,1)S(1)} %copy-done, f32[256]{0:T(256)S(1)} %bitcast.195, s32[256]{0:T(256)S(1)} %add.353), kind=kOutput, calls=%fused_computation.82 | convolution fusion | flops 369426432 | bytes 2754560 | tf_op jit(solution)/shard_map/dot_general | solution.py:84
  8.6 4.8 %collective-permute-start.2 = (bf16[256,256]{1,0:T(8,128)(2,1)S(1)}, bf16[256,256]{1,0:T(8,128)(2,1)S(1)}, u32[]{:S(2)}, u32[]{:S(2)}) collective-permute-start(bf16[256,256]{1,0:T(8,128)(2,1)S(1)} %convolution_convert_fusion.3), channel_id=1, source_target_pairs={{0,32},{32,64},{64,96},{96,128},{128,160},{160,192},{192,224},{1,3... | collective-permute-start | bytes 393224 | tf_op jit(solution)/shard_map/ppermute | solution.py:19
  13.6 9.0 %collective-permute-done = bf16[128,2560]{1,0:T(8,128)(2,1)} collective-permute-done((bf16[128,2560]{1,0:T(8,128)(2,1)S(1)}, bf16[128,2560]{1,0:T(8,128)(2,1)}, u32[]{:S(2)}, u32[]{:S(2)}) %collective-permute-start) | collective-permute-done | bytes 655392 | tf_op jit(solution)/shard_map/ppermute | solution.py:27
  35.6 2.5 %convolution_convert_fusion.2 = bf16[256,256]{1,0:T(8,128)(2,1)S(1)} fusion(bf16[1,2560,256]{2,1,0:T(8,128)(2,1)} %param.7, bf16[128,2560]{1,0:T(8,128)(2,1)} %copy-done.22, bf16[128,2560]{1,0:T(8,128)(2,1)} %collective-permute-done, bf16[256,128]{1,0:T(8,128)(2,1)S(1)} %get-tuple-element.85, bf16[256,128]{1,0:T(8,128)(2,1)S(1)} %get-tuple-element.84, ...), kind=kOutput, calls=%fused_computation.81 | convolution fusion | flops 372441088 | bytes 2885633 | tf_op jit(solution)/shard_map/dot_general | solution.py:84
  41.1 6.5 %collective-permute-start.5 = (bf16[256,256]{1,0:T(8,128)(2,1)S(1)}, bf16[256,256]{1,0:T(8,128)(2,1)S(1)}, u32[]{:S(2)}, u32[]{:S(2)}) collective-permute-start(bf16[256,256]{1,0:T(8,128)(2,1)S(1)} %convolution_convert_fusion.2), channel_id=1, source_target_pairs={{0,32},{32,64},{64,96},{96,128},{128,160},{160,192},{192,224},{1,3... | collective-permute-start | bytes 393224 | tf_op jit(solution)/shard_map/ppermute | solution.py:19
  49.9 2.8 %collective-permute-done.6 = bf16[256,256]{1,0:T(8,128)(2,1)S(1)} collective-permute-done((bf16[256,256]{1,0:T(8,128)(2,1)S(1)}, bf16[256,256]{1,0:T(8,128)(2,1)S(1)}, u32[]{:S(2)}, u32[]{:S(2)}) %collective-permute-start.6) | collective-permute-done | bytes 131104 | tf_op jit(solution)/shard_map/ppermute | solution.py:19
  54.0 2.0 %convolution_subtract_fusion = f32[256,2560]{1,0:T(8,128)S(1)} fusion(f32[256,2560]{1,0:T(8,128)S(1)} %fusion.157, bf16[256,256]{1,0:T(8,128)(2,1)S(1)} %convolution_convert_fusion.2, bf16[1,4,256,2560]{3,2,1,0:T(8,128)(2,1)} %param.9), kind=kOutput, calls=%fused_computation.9 | convolution fusion | flops 336199680 | bytes 6684672 | tf_op jit(solution)/shard_map/dot_general | solution.py:88
  58.0 2.1 %collective-permute-done.10 = bf16[128,2560]{1,0:T(8,128)(2,1)S(1)} collective-permute-done((bf16[128,2560]{1,0:T(8,128)(2,1)S(1)}, bf16[128,2560]{1,0:T(8,128)(2,1)S(1)}, u32[]{:S(2)}, u32[]{:S(2)}) %collective-permute-start.10) | collective-permute-done | bytes 655392 | tf_op jit(solution)/shard_map/ppermute | solution.py:23
  63.8 4.7 %collective-permute-start.12 = (bf16[16,2560]{1,0:T(8,128)(2,1)S(1)}, bf16[16,2560]{1,0:T(8,128)(2,1)S(1)}, u32[]{:S(2)}, u32[]{:S(2)}) collective-permute-start(bf16[16,2560]{1,0:T(8,128)(2,1)S(1)} %slice.199), channel_id=1, source_target_pairs={{0,8},{2,26},{4,12},{6,30},{8,16},{10,2},{12,20},{14,6},{16,24},{1... | collective-permute-start | bytes 245768 | tf_op jit(solution)/shard_map/ppermute | solution.py:35
  70.1 2.5 %collective-permute-done.12 = bf16[16,2560]{1,0:T(8,128)(2,1)S(1)} collective-permute-done((bf16[16,2560]{1,0:T(8,128)(2,1)S(1)}, bf16[16,2560]{1,0:T(8,128)(2,1)S(1)}, u32[]{:S(2)}, u32[]{:S(2)}) %collective-permute-start.12) | collective-permute-done | bytes 81952 | tf_op jit(solution)/shard_map/ppermute | solution.py:35
  73.7 2.0 %collective-permute-start.14 = (bf16[32,2560]{1,0:T(8,128)(2,1)S(1)}, bf16[32,2560]{1,0:T(8,128)(2,1)S(1)}, u32[]{:S(2)}, u32[]{:S(2)}) collective-permute-start(bf16[32,2560]{1,0:T(8,128)(2,1)S(1)} %pad_maximum_fusion.8), channel_id=1, source_target_pairs={{0,8},{2,26},{4,12},{6,30},{8,16},{10,2},{12,20},{14,6},{16,24},{1... | collective-permute-start | bytes 491528 | tf_op jit(solution)/shard_map/ppermute | solution.py:35
  75.9 5.4 %collective-permute-done.14 = bf16[32,2560]{1,0:T(8,128)(2,1)S(1)} collective-permute-done((bf16[32,2560]{1,0:T(8,128)(2,1)S(1)}, bf16[32,2560]{1,0:T(8,128)(2,1)S(1)}, u32[]{:S(2)}, u32[]{:S(2)}) %collective-permute-start.14) | collective-permute-done | bytes 163872 | tf_op jit(solution)/shard_map/ppermute | solution.py:35
  84.1 4.0 %collective-permute-start.16 = (bf16[32,2560]{1,0:T(8,128)(2,1)S(1)}, bf16[32,2560]{1,0:T(8,128)(2,1)S(1)}, u32[]{:S(2)}, u32[]{:S(2)}) collective-permute-start(bf16[32,2560]{1,0:T(8,128)(2,1)S(1)} %fusion.139), channel_id=1, source_target_pairs={{0,24},{2,10},{4,28},{6,14},{8,0},{10,18},{12,4},{14,22},{16,8},{1... | collective-permute-start | bytes 491528 | tf_op jit(solution)/shard_map/ppermute | solution.py:35
  89.4 3.3 %collective-permute-done.16 = bf16[32,2560]{1,0:T(8,128)(2,1)S(1)} collective-permute-done((bf16[32,2560]{1,0:T(8,128)(2,1)S(1)}, bf16[32,2560]{1,0:T(8,128)(2,1)S(1)}, u32[]{:S(2)}, u32[]{:S(2)}) %collective-permute-start.16) | collective-permute-done | bytes 163872 | tf_op jit(solution)/shard_map/ppermute | solution.py:35
  92.7 4.7 %collective-permute-start.18 = (bf16[16,2560]{1,0:T(8,128)(2,1)S(1)}, bf16[16,2560]{1,0:T(8,128)(2,1)S(1)}, u32[]{:S(2)}, u32[]{:S(2)}) collective-permute-start(bf16[16,2560]{1,0:T(8,128)(2,1)S(1)} %slice.180), channel_id=1, source_target_pairs={{0,24},{2,10},{4,28},{6,14},{8,0},{10,18},{12,4},{14,22},{16,8},{1... | collective-permute-start | bytes 245768 | tf_op jit(solution)/shard_map/ppermute | solution.py:35
  99.5 5.6 %collective-permute-done.19 = bf16[48,2560]{1,0:T(8,128)(2,1)S(1)} collective-permute-done((bf16[48,2560]{1,0:T(8,128)(2,1)S(1)}, bf16[48,2560]{1,0:T(8,128)(2,1)S(1)}, u32[]{:S(2)}, u32[]{:S(2)}) %collective-permute-start.19) | collective-permute-done | bytes 245792 | tf_op jit(solution)/shard_map/ppermute | solution.py:27
  105.5 2.1 %collective-permute-done.20 = bf16[128,2560]{1,0:T(8,128)(2,1)S(1)} collective-permute-done((bf16[128,2560]{1,0:T(8,128)(2,1)S(1)}, bf16[128,2560]{1,0:T(8,128)(2,1)S(1)}, u32[]{:S(2)}, u32[]{:S(2)}) %collective-permute-start.20) | collective-permute-done | bytes 655392 | tf_op jit(solution)/shard_map/ppermute | solution.py:23
  109.4 5.7 %collective-permute-start.23 = (bf16[512,256]{1,0:T(8,128)(2,1)S(1)}, bf16[512,256]{1,0:T(8,128)(2,1)S(1)}, u32[]{:S(2)}, u32[]{:S(2)}) collective-permute-start(bf16[512,256]{1,0:T(8,128)(2,1)S(1)} %pad_maximum_fusion.5), channel_id=1, source_target_pairs={{64,0},{96,32},{128,64},{160,96},{192,128},{224,160},{65,1},{97,33... | collective-permute-start | bytes 786440 | tf_op jit(solution)/shard_map/ppermute | solution.py:19
  115.7 5.3 %collective-permute-done.23 = bf16[512,256]{1,0:T(8,128)(2,1)S(1)} collective-permute-done((bf16[512,256]{1,0:T(8,128)(2,1)S(1)}, bf16[512,256]{1,0:T(8,128)(2,1)S(1)}, u32[]{:S(2)}, u32[]{:S(2)}) %collective-permute-start.23) | collective-permute-done | bytes 262176 | tf_op jit(solution)/shard_map/ppermute | solution.py:19
  121.8 2.0 %collective-permute-done.22 = bf16[128,2560]{1,0:T(8,128)(2,1)S(1)} collective-permute-done((bf16[128,2560]{1,0:T(8,128)(2,1)S(1)}, bf16[128,2560]{1,0:T(8,128)(2,1)S(1)}, u32[]{:S(2)}, u32[]{:S(2)}) %collective-permute-start.22) | collective-permute-done | bytes 655392 | tf_op jit(solution)/shard_map/ppermute | solution.py:23
  126.7 4.4 %collective-permute-start.25 = (bf16[256,256]{1,0:T(8,128)(2,1)S(1)}, bf16[256,256]{1,0:T(8,128)(2,1)S(1)}, u32[]{:S(2)}, u32[]{:S(2)}) collective-permute-start(bf16[256,256]{1,0:T(8,128)(2,1)S(1)} %fusion.95), channel_id=1, source_target_pairs={{64,0},{96,32},{128,64},{160,96},{192,128},{224,160},{65,1},{97,33... | collective-permute-start | bytes 393224 | tf_op jit(solution)/shard_map/ppermute | solution.py:19
  131.1 3.7 %collective-permute-start.26 = (bf16[256,256]{1,0:T(8,128)(2,1)S(1)}, bf16[256,256]{1,0:T(8,128)(2,1)S(1)}, u32[]{:S(2)}, u32[]{:S(2)}) collective-permute-start(bf16[256,256]{1,0:T(8,128)(2,1)S(1)} %fusion.92), channel_id=1, source_target_pairs={{96,0},{128,32},{160,64},{192,96},{224,128},{97,1},{129,33},{161,6... | collective-permute-start | bytes 393224 | tf_op jit(solution)/shard_map/ppermute | solution.py:19
  134.7 4.8 %collective-permute-start.24 = (bf16[512,256]{1,0:T(8,128)(2,1)S(1)}, bf16[512,256]{1,0:T(8,128)(2,1)S(1)}, u32[]{:S(2)}, u32[]{:S(2)}) collective-permute-start(bf16[512,256]{1,0:T(8,128)(2,1)S(1)} %pad_maximum_fusion.6), channel_id=1, source_target_pairs={{32,0},{64,32},{96,64},{128,96},{160,128},{192,160},{224,192},{33,... | collective-permute-start | bytes 786440 | tf_op jit(solution)/shard_map/ppermute | solution.py:19
  143.8 2.9 %maximum_bitcast_fusion = bf16[1,4,256,2560]{3,2,1,0:T(8,128)(2,1)} fusion(bf16[1,256,2560]{2,1,0:T(8,128)(2,1)S(1)} %fusion.11, bf16[1,256,2560]{2,1,0:T(8,128)(2,1)S(1)} %fusion.10, bf16[1,256,2560]{2,1,0:T(8,128)(2,1)S(1)} %fusion.9, bf16[1,256,2560]{2,1,0:T(8,128)(2,1)S(1)} %fusion.8), kind=kLoop, calls=%fused_computation.1 | loop fusion | flops 7864320 | bytes 10485760 | tf_op jit(solution)/shard_map/broadcast_in_dim | solution.py:187
  (189 shorter events, 52.1 us)
Async XLA Ops:
  2.0 20.6 %collective-permute-start = (bf16[128,2560]{1,0:T(8,128)(2,1)S(1)}, bf16[128,2560]{1,0:T(8,128)(2,1)}, u32[]{:S(2)}, u32[]{:S(2)}) collective-permute-start(bf16[128,2560]{1,0:T(8,128)(2,1)S(1)} %dynamic-slice_bitcast_fusion), channel_id=1, source_target_pairs={{0,1},{1,0},{2,3},{3,2},{4,5},{5,4},{6,7},{7,6},{8,9},{9,8},{10,11... | collective-permute-start | bytes 1966088 | tf_op jit(solution)/shard_map/ppermute | solution.py:27
  6.0 21.8 %collective-permute-start.4 = (bf16[256,256]{1,0:T(8,128)(2,1)S(1)}, bf16[256,256]{1,0:T(8,128)(2,1)S(1)}, u32[]{:S(2)}, u32[]{:S(2)}) collective-permute-start(bf16[256,256]{1,0:T(8,128)(2,1)S(1)} %convolution_convert_fusion.3), channel_id=1, source_target_pairs={{0,96},{32,128},{64,160},{96,192},{128,224},{1,97},{33,129},{65,16... | collective-permute-start | bytes 393224 | tf_op jit(solution)/shard_map/ppermute | solution.py:19
  7.3 19.5 %collective-permute-start.3 = (bf16[256,256]{1,0:T(8,128)(2,1)S(1)}, bf16[256,256]{1,0:T(8,128)(2,1)S(1)}, u32[]{:S(2)}, u32[]{:S(2)}) collective-permute-start(bf16[256,256]{1,0:T(8,128)(2,1)S(1)} %convolution_convert_fusion.3), channel_id=1, source_target_pairs={{0,64},{32,96},{64,128},{96,160},{128,192},{160,224},{1,65},{33,97... | collective-permute-start | bytes 393224 | tf_op jit(solution)/shard_map/ppermute | solution.py:19
  8.6 17.3 %collective-permute-start.2 = (bf16[256,256]{1,0:T(8,128)(2,1)S(1)}, bf16[256,256]{1,0:T(8,128)(2,1)S(1)}, u32[]{:S(2)}, u32[]{:S(2)}) collective-permute-start(bf16[256,256]{1,0:T(8,128)(2,1)S(1)} %convolution_convert_fusion.3), channel_id=1, source_target_pairs={{0,32},{32,64},{64,96},{96,128},{128,160},{160,192},{192,224},{1,3... | collective-permute-start | bytes 393224 | tf_op jit(solution)/shard_map/ppermute | solution.py:19
  25.9 5.0 %collective-permute-start.1 = (bf16[128,2560]{1,0:T(8,128)(2,1)}, bf16[128,2560]{1,0:T(8,128)(2,1)S(1)}, u32[]{:S(2)}, u32[]{:S(2)}) collective-permute-start(bf16[128,2560]{1,0:T(8,128)(2,1)} %collective-permute-done), channel_id=1, source_target_pairs={{0,2},{2,0},{4,6},{6,4},{8,10},{10,8},{12,14},{14,12},{16,18},{18,... | collective-permute-start | bytes 1966088 | tf_op jit(solution)/shard_map/ppermute | solution.py:23
  30.2 2.3 %collective-permute-start.8 = (bf16[128,2560]{1,0:T(8,128)(2,1)S(1)}, bf16[128,2560]{1,0:T(8,128)(2,1)S(1)}, u32[]{:S(2)}, u32[]{:S(2)}) collective-permute-start(bf16[128,2560]{1,0:T(8,128)(2,1)S(1)} %slice.318), channel_id=1, source_target_pairs={{0,2},{2,0},{4,6},{6,4},{8,10},{10,8},{12,14},{14,12},{16,18},{18,... | collective-permute-start | bytes 1966088 | tf_op jit(solution)/shard_map/ppermute | solution.py:23
  34.0 20.1 %collective-permute-start.9 = (bf16[80,2560]{1,0:T(8,128)(2,1)S(1)}, bf16[80,2560]{1,0:T(8,128)(2,1)S(1)}, u32[]{:S(2)}, u32[]{:S(2)}) collective-permute-start(bf16[80,2560]{1,0:T(8,128)(2,1)S(1)} %slice.193), channel_id=1, source_target_pairs={{0,1},{1,0},{2,3},{3,2},{4,5},{5,4},{6,7},{7,6},{8,9},{9,8},{10,11... | collective-permute-start | bytes 1228808 | tf_op jit(solution)/shard_map/ppermute | solution.py:27
  38.2 11.7 %collective-permute-start.7 = (bf16[256,256]{1,0:T(8,128)(2,1)S(1)}, bf16[256,256]{1,0:T(8,128)(2,1)S(1)}, u32[]{:S(2)}, u32[]{:S(2)}) collective-permute-start(bf16[256,256]{1,0:T(8,128)(2,1)S(1)} %convolution_convert_fusion.2), channel_id=1, source_target_pairs={{0,96},{32,128},{64,160},{96,192},{128,224},{1,97},{33,129},{65,16... | collective-permute-start | bytes 393224 | tf_op jit(solution)/shard_map/ppermute | solution.py:19
  39.8 12.9 %collective-permute-start.6 = (bf16[256,256]{1,0:T(8,128)(2,1)S(1)}, bf16[256,256]{1,0:T(8,128)(2,1)S(1)}, u32[]{:S(2)}, u32[]{:S(2)}) collective-permute-start(bf16[256,256]{1,0:T(8,128)(2,1)S(1)} %convolution_convert_fusion.2), channel_id=1, source_target_pairs={{0,64},{32,96},{64,128},{96,160},{128,192},{160,224},{1,65},{33,97... | collective-permute-start | bytes 393224 | tf_op jit(solution)/shard_map/ppermute | solution.py:19
  41.1 12.9 %collective-permute-start.5 = (bf16[256,256]{1,0:T(8,128)(2,1)S(1)}, bf16[256,256]{1,0:T(8,128)(2,1)S(1)}, u32[]{:S(2)}, u32[]{:S(2)}) collective-permute-start(bf16[256,256]{1,0:T(8,128)(2,1)S(1)} %convolution_convert_fusion.2), channel_id=1, source_target_pairs={{0,32},{32,64},{64,96},{96,128},{128,160},{160,192},{192,224},{1,3... | collective-permute-start | bytes 393224 | tf_op jit(solution)/shard_map/ppermute | solution.py:19
  57.9 2.2 %collective-permute-start.10 = (bf16[128,2560]{1,0:T(8,128)(2,1)S(1)}, bf16[128,2560]{1,0:T(8,128)(2,1)S(1)}, u32[]{:S(2)}, u32[]{:S(2)}) collective-permute-start(bf16[128,2560]{1,0:T(8,128)(2,1)S(1)} %slice.317), channel_id=1, source_target_pairs={{0,2},{2,0},{4,6},{6,4},{8,10},{10,8},{12,14},{14,12},{16,18},{18,... | collective-permute-start | bytes 1966088 | tf_op jit(solution)/shard_map/ppermute | solution.py:23
  61.0 11.6 %collective-permute-start.11 = (bf16[64,2560]{1,0:T(8,128)(2,1)}, bf16[64,2560]{1,0:T(8,128)(2,1)}, u32[]{:S(2)}, u32[]{:S(2)}) collective-permute-start(bf16[64,2560]{1,0:T(8,128)(2,1)} %slice.198), channel_id=1, source_target_pairs={{0,4},{2,30},{4,8},{6,2},{8,12},{10,6},{12,16},{14,10},{16,20},{18... | collective-permute-start | bytes 983048 | tf_op jit(solution)/shard_map/ppermute | solution.py:35
  63.7 6.4 %collective-permute-start.13 = (bf16[48,2560]{1,0:T(8,128)(2,1)}, bf16[48,2560]{1,0:T(8,128)(2,1)S(1)}, u32[]{:S(2)}, u32[]{:S(2)}) collective-permute-start(bf16[48,2560]{1,0:T(8,128)(2,1)} %slice.200), channel_id=1, source_target_pairs={{0,1},{1,0},{2,3},{3,2},{4,5},{5,4},{6,7},{7,6},{8,9},{9,8},{10,11... | collective-permute-start | bytes 737288 | tf_op jit(solution)/shard_map/ppermute | solution.py:27
  63.8 8.8 %collective-permute-start.12 = (bf16[16,2560]{1,0:T(8,128)(2,1)S(1)}, bf16[16,2560]{1,0:T(8,128)(2,1)S(1)}, u32[]{:S(2)}, u32[]{:S(2)}) collective-permute-start(bf16[16,2560]{1,0:T(8,128)(2,1)S(1)} %slice.199), channel_id=1, source_target_pairs={{0,8},{2,26},{4,12},{6,30},{8,16},{10,2},{12,20},{14,6},{16,24},{1... | collective-permute-start | bytes 245768 | tf_op jit(solution)/shard_map/ppermute | solution.py:35
  73.7 7.6 %collective-permute-start.14 = (bf16[32,2560]{1,0:T(8,128)(2,1)S(1)}, bf16[32,2560]{1,0:T(8,128)(2,1)S(1)}, u32[]{:S(2)}, u32[]{:S(2)}) collective-permute-start(bf16[32,2560]{1,0:T(8,128)(2,1)S(1)} %pad_maximum_fusion.8), channel_id=1, source_target_pairs={{0,8},{2,26},{4,12},{6,30},{8,16},{10,2},{12,20},{14,6},{16,24},{1... | collective-permute-start | bytes 491528 | tf_op jit(solution)/shard_map/ppermute | solution.py:35
  84.1 8.6 %collective-permute-start.16 = (bf16[32,2560]{1,0:T(8,128)(2,1)S(1)}, bf16[32,2560]{1,0:T(8,128)(2,1)S(1)}, u32[]{:S(2)}, u32[]{:S(2)}) collective-permute-start(bf16[32,2560]{1,0:T(8,128)(2,1)S(1)} %fusion.139), channel_id=1, source_target_pairs={{0,24},{2,10},{4,28},{6,14},{8,0},{10,18},{12,4},{14,22},{16,8},{1... | collective-permute-start | bytes 491528 | tf_op jit(solution)/shard_map/ppermute | solution.py:35
  92.7 6.7 %collective-permute-start.18 = (bf16[16,2560]{1,0:T(8,128)(2,1)S(1)}, bf16[16,2560]{1,0:T(8,128)(2,1)S(1)}, u32[]{:S(2)}, u32[]{:S(2)}) collective-permute-start(bf16[16,2560]{1,0:T(8,128)(2,1)S(1)} %slice.180), channel_id=1, source_target_pairs={{0,24},{2,10},{4,28},{6,14},{8,0},{10,18},{12,4},{14,22},{16,8},{1... | collective-permute-start | bytes 245768 | tf_op jit(solution)/shard_map/ppermute | solution.py:35
  97.4 7.6 %collective-permute-start.17 = (bf16[64,2560]{1,0:T(8,128)(2,1)S(1)}, bf16[64,2560]{1,0:T(8,128)(2,1)S(1)}, u32[]{:S(2)}, u32[]{:S(2)}) collective-permute-start(bf16[64,2560]{1,0:T(8,128)(2,1)S(1)} %pad_maximum_fusion.4), channel_id=1, source_target_pairs={{0,28},{2,6},{4,0},{6,10},{8,4},{10,14},{12,8},{14,18},{16,12},{18... | collective-permute-start | bytes 983048 | tf_op jit(solution)/shard_map/ppermute | solution.py:35
  97.4 7.6 %collective-permute-start.19 = (bf16[48,2560]{1,0:T(8,128)(2,1)S(1)}, bf16[48,2560]{1,0:T(8,128)(2,1)S(1)}, u32[]{:S(2)}, u32[]{:S(2)}) collective-permute-start(bf16[48,2560]{1,0:T(8,128)(2,1)S(1)} %pad_maximum_fusion.7), channel_id=1, source_target_pairs={{0,1},{1,0},{2,3},{3,2},{4,5},{5,4},{6,7},{7,6},{8,9},{9,8},{10,11... | collective-permute-start | bytes 737288 | tf_op jit(solution)/shard_map/ppermute | solution.py:27
  105.1 16.5 %collective-permute-start.21 = (bf16[80,2560]{1,0:T(8,128)(2,1)S(1)}, bf16[80,2560]{1,0:T(8,128)(2,1)S(1)}, u32[]{:S(2)}, u32[]{:S(2)}) collective-permute-start(bf16[80,2560]{1,0:T(8,128)(2,1)S(1)} %pad_maximum_fusion.2), channel_id=1, source_target_pairs={{0,1},{1,0},{2,3},{3,2},{4,5},{5,4},{6,7},{7,6},{8,9},{9,8},{10,11... | collective-permute-start | bytes 1228808 | tf_op jit(solution)/shard_map/ppermute | solution.py:27
  109.4 11.6 %collective-permute-start.23 = (bf16[512,256]{1,0:T(8,128)(2,1)S(1)}, bf16[512,256]{1,0:T(8,128)(2,1)S(1)}, u32[]{:S(2)}, u32[]{:S(2)}) collective-permute-start(bf16[512,256]{1,0:T(8,128)(2,1)S(1)} %pad_maximum_fusion.5), channel_id=1, source_target_pairs={{64,0},{96,32},{128,64},{160,96},{192,128},{224,160},{65,1},{97,33... | collective-permute-start | bytes 786440 | tf_op jit(solution)/shard_map/ppermute | solution.py:19
  126.7 20.1 %collective-permute-start.25 = (bf16[256,256]{1,0:T(8,128)(2,1)S(1)}, bf16[256,256]{1,0:T(8,128)(2,1)S(1)}, u32[]{:S(2)}, u32[]{:S(2)}) collective-permute-start(bf16[256,256]{1,0:T(8,128)(2,1)S(1)} %fusion.95), channel_id=1, source_target_pairs={{64,0},{96,32},{128,64},{160,96},{192,128},{224,160},{65,1},{97,33... | collective-permute-start | bytes 393224 | tf_op jit(solution)/shard_map/ppermute | solution.py:19
  131.1 15.7 %collective-permute-start.26 = (bf16[256,256]{1,0:T(8,128)(2,1)S(1)}, bf16[256,256]{1,0:T(8,128)(2,1)S(1)}, u32[]{:S(2)}, u32[]{:S(2)}) collective-permute-start(bf16[256,256]{1,0:T(8,128)(2,1)S(1)} %fusion.92), channel_id=1, source_target_pairs={{96,0},{128,32},{160,64},{192,96},{224,128},{97,1},{129,33},{161,6... | collective-permute-start | bytes 393224 | tf_op jit(solution)/shard_map/ppermute | solution.py:19
  134.7 12.0 %collective-permute-start.24 = (bf16[512,256]{1,0:T(8,128)(2,1)S(1)}, bf16[512,256]{1,0:T(8,128)(2,1)S(1)}, u32[]{:S(2)}, u32[]{:S(2)}) collective-permute-start(bf16[512,256]{1,0:T(8,128)(2,1)S(1)} %pad_maximum_fusion.6), channel_id=1, source_target_pairs={{32,0},{64,32},{96,64},{128,96},{160,128},{192,160},{224,192},{33,... | collective-permute-start | bytes 786440 | tf_op jit(solution)/shard_map/ppermute | solution.py:19
  (33 other events, 297.4 us)

commit v3 on v2

--- a/solution.py
+++ b/solution.py
@@ -33,6 +33,16 @@
         route.append((z * CORES, (z + distance) % Z * CORES))
         route.append((z * CORES + 1, (z - distance) % Z * CORES + 1))
     return lax.ppermute(block, "latent", route)
+
+
+def to_owner(block):
+    route = []
+    for z in range(Z):
+        for core in range(CORES):
+            for dp in range(2):
+                token_block = (1 - dp) * Z * CORES + z * CORES + core
+                route.append((token_block, (z * CORES + core) * 2 + dp))
+    return lax.ppermute(block, ("latent", "dp"), route)
 
 
 def block_order(core, z):
@@ -72,20 +82,12 @@
     token = (order[:, None] * piece + jnp.arange(piece)[None, :]).reshape(half)
     shuffle = (token[:, None] == jnp.arange(half)[None, :]).astype(BF16)
     swapped = jnp.where(core == 0, shuffle, jnp.roll(shuffle, group, axis=1))
-    own_row = token[:, None] - (2 * latent + dp) % (2 * Z) * piece == jnp.arange(piece)[None, :]
-    is_near = latent // Z == dp
-    near_mark = (own_row & is_near).astype(BF16)
-    far_mark = (own_row & ~is_near).astype(BF16)
-    own_targets = targets[:, 0]
+    own_targets = to_owner(targets[:, 0])
 
     def encode(rows, place):
         preact = jnp.dot(rows, enc_weight, preferred_element_type=F32) + b_enc[0]
         natural = jnp.maximum(preact, 0.0).astype(BF16)
         return jnp.dot(place, natural, preferred_element_type=F32).astype(BF16)
-
-    def decode_first(source, mark):
-        own = jnp.dot(mark, own_targets, preferred_element_type=F32)
-        return jnp.dot(source, weights[0], preferred_element_type=F32) - own
 
     def decode_rest(total, sources):
         for k in range(1, reach_count):
@@ -98,9 +100,10 @@
 
     cut = 3 * piece
     near = spread(encode(x, shuffle))
-    near[0], near_mark, far_x0 = lax.optimization_barrier((near[0], near_mark, far_x0))
-    near_sum = decode_first(near[0], near_mark)
-    far_x1 = over_core(after(far_x0, near_sum))
+    near[0], far_x0 = lax.optimization_barrier((near[0], far_x0))
+    near_sum = jnp.dot(near[0], weights[0], preferred_element_type=F32)
+    far_x0, near_sum, own_targets = lax.optimization_barrier((far_x0, near_sum, own_targets))
+    far_x1 = over_core(far_x0)
     near_sum = decode_rest(near_sum, near)
     near_part = near_sum[:group] + over_core(near_sum[group:].astype(BF16)).astype(F32)
     near_part = near_part.astype(BF16)
@@ -109,8 +112,10 @@
 
     far_x1 = after(far_x1, near_sum)
     far = spread(encode(jnp.concatenate([far_x0, far_x1], axis=0), swapped))
-    *far, from_dp1 = lax.optimization_barrier((*far, from_dp1))
-    far_sum = decode_rest(decode_first(far[0], far_mark), far)
+    norms = jnp.sqrt(jnp.sum(jnp.square(weights.astype(F32)), axis=2) + EPSILON)
+    *far, from_dp1, norms = lax.optimization_barrier((*far, from_dp1, norms))
+    far_sum = jnp.dot(far[0], weights[0], preferred_element_type=F32)
+    far_sum = decode_rest(far_sum, far)
     part = far_sum[:group] + over_core(far_sum[group:].astype(BF16)).astype(F32)
     away = (part[cut:] + from_dp1.astype(F32)).astype(BF16)
     by_one = over_z(away[: 4 * piece], 1)
@@ -120,13 +125,12 @@
     passing = home[piece:] + by_one[: 2 * piece].astype(F32)
     passing = jnp.concatenate([passing[:piece] + by_two.astype(F32), passing[piece:]], axis=0)
     got = over_z(passing.astype(BF16), 2).astype(F32) + by_one[2 * piece :].astype(F32)
-    got = jnp.concatenate([got[:piece] + home[:piece], got[piece:]], axis=0)
+    own = got[:piece] + home[:piece] - own_targets.astype(F32)
+    got = jnp.concatenate([own, got[piece:]], axis=0)
     other = over_core(got)
     misfit = got + jnp.concatenate([other[piece:], other[:piece]], axis=0)
     pair = (misfit * loss_scale).astype(BF16)
 
-    later_weights, pair = lax.optimization_barrier((weights, pair))
-    norms = jnp.sqrt(jnp.sum(jnp.square(later_weights.astype(F32)), axis=2) + EPSILON)
     scales = []
     for k in range(reach_count):
         mass = jnp.sum(near[k].astype(F32), axis=0) + jnp.sum(far[k].astype(F32), axis=0)
@@ -160,31 +164,37 @@
         return terms
 
     far_terms = back(far_g0, far_g1)
-    far_two = jnp.concatenate([term.astype(BF16) for term in far_terms[2:]], axis=0)
-    far_down = over_layers(far_two, -2).astype(F32)
-    far_step = (far_terms[1] + far_down[half:]).astype(BF16)
+    far_down = over_layers(far_terms[3].astype(BF16), -2).astype(F32)
     far_g = jnp.concatenate([far_g0, far_g1], axis=0)
+    bases = []
+    for k in range(reach_count):
+        base = lax.dot_general(
+            far[k], far_g, (((0,), (0,)), ((), ())), preferred_element_type=F32
+        )
+        bases.append(base + scales[k][:, None] * weights[k].astype(F32))
     near_early, near_late = lax.optimization_barrier((near_early, near_late, far_terms))[:2]
     near_g0 = jnp.concatenate([near_early, near_late], axis=0)
-    near_g1 = over_core(near_g0)
+    near_g1, *bases = lax.optimization_barrier((over_core(near_g0), *bases))
     near_g = jnp.concatenate([near_g0, near_g1], axis=0)
     near_terms = back(near_g0, near_g1)
+    far_down = after(far_down, near_terms)
+    far_step = (far_terms[1] + far_down).astype(BF16)
     near_down3 = over_layers(near_terms[3].astype(BF16), -3).astype(F32)
     step = over_layers(jnp.concatenate([near_terms[1].astype(BF16), far_step], axis=0), -1)
-    near_down2 = over_layers(near_terms[2].astype(BF16), -2).astype(F32)
-    near_up = near_terms[0] + step[:half].astype(F32) + near_down2 + near_down3
-    far_up = far_terms[0] + step[half:].astype(F32) + far_down[:half]
+    two_down = jnp.concatenate([near_terms[2], far_terms[2]], axis=0).astype(BF16)
+    two_down = over_layers(two_down, -2).astype(F32)
+    near_up = near_terms[0] + step[:half].astype(F32) + two_down[:half] + near_down3
+    far_up = far_terms[0] + step[half:].astype(F32) + two_down[half:]
     upward = jnp.concatenate([far_up, near_up], axis=0)
-    pieces = []
+    grad_dec = jnp.zeros(w_dec.shape, BF16)
+    grad_dec = after(grad_dec, far_g)
     for k in range(reach_count):
-        contrib = lax.dot_general(
-            far[k], far_g, (((0,), (0,)), ((), ())), preferred_element_type=F32
-        ) + lax.dot_general(
+        contrib = bases[k] + lax.dot_general(
             near[k], near_g, (((0,), (0,)), ((), ())), preferred_element_type=F32
         )
-        contrib = contrib + scales[k][:, None] * weights[k].astype(F32)
-        pieces.append(contrib.astype(BF16))
-    grad_dec = jnp.stack(pieces)[None]
+        grad_dec = lax.dynamic_update_slice(
+            grad_dec, contrib.astype(BF16)[None, None], (0, k, 0, 0)
+        )
     out = jnp.concatenate([upward, upward[:half]], axis=0)
     out = lax.dynamic_slice_in_dim(out, (1 - dp) * half, 2 * half, 0)[:, None, :]
     return (grad_dec, out)

time: 152 us -> 146 us (0.961)
  other arithmetic: 10.8 us -> 5.35 us
    ppermute x10, starting transfers between devices: 35.3 us -> 29.7 us  [over_layers(): return lax.ppermute(block, 'layer', route)]
    ppermute x10, waiting for transfers between devices: 11.2 us -> 16.4 us  [over_layers(): return lax.ppermute(block, 'layer', route)]
    ppermute x6, waiting for transfers between devices: 9.13 us -> 4.26 us  [over_core(): return lax.ppermute(block, 'latent', [(i, i ^ 1) for i in range(Z * CORES)])]
    ppermute x6, waiting for transfers between devices: 13 us -> 17.6 us  [over_z(): return lax.ppermute(block, 'latent', route)]
    ppermute x5, waiting for transfers between devices: 15.2 us -> 10.7 us  [over_dp(): return lax.ppermute(block, 'dp', [(0, 1), (1, 0)])]
    ppermute x6, starting transfers between devices: 0.93 us -> 3.98 us  [over_core(): return lax.ppermute(block, 'latent', [(i, i ^ 1) for i in range(Z * CORES)])]
    broadcast_in_dim x1 -> x0, other arithmetic: 2.94 us -> none  [shards(): grad_dec = jnp.stack(pieces)[None]]
    dot_general x6, matrix products: 3.14 us -> 5.89 us  [decode_rest(): total = total + jnp.dot(source, weights[k], preferred_element_type=F32)]
  transfers between devices with their start and end apart: 27 -> 28, of which waited for: 16 -> 14; matrix products, arithmetic and copies ran while one was open for 16% -> 15% of each run, Pallas kernels for 0% -> 0%
where the time goes in v3:
time: 146 us; the launch traced here: 144 us
  starting transfers between devices  58.7 us (40%)
  waiting for transfers between devices  49 us (34%)
  matrix products  24 us (16%)
  local copies, waits for them, and re-layouts  5.84 us (4%)
  other arithmetic  5.35 us (4%)
    ppermute x10, starting transfers between devices, over_layers(): return lax.ppermute(block, 'layer', route)  29.7 us
    ppermute x6, starting transfers between devices, over_z(): return lax.ppermute(block, 'latent', route)  18.7 us
    ppermute x6, waiting for transfers between devices, over_z(): return lax.ppermute(block, 'latent', route)  17.6 us
    ppermute x10, waiting for transfers between devices, over_layers(): return lax.ppermute(block, 'layer', route)  16.4 us
    ppermute x5, waiting for transfers between devices, over_dp(): return lax.ppermute(block, 'dp', [(0, 1), (1, 0)])  10.7 us
    dot_general x6, matrix products, decode_rest(): total = total + jnp.dot(source, weights[k], preferred_element_type=F32)  5.89 us
    ppermute x5, starting transfers between devices, over_dp(): return lax.ppermute(block, 'dp', [(0, 1), (1, 0)])  4.73 us
    dot_general x2, matrix products, encode(): return jnp.dot(place, natural, preferred_element_type=F32).astype(BF16)  4.68 us
  transfers between devices with their start and end apart: 28, of which 14 were waited for; matrix products, arithmetic and copies ran while one was open for 15% of the time, Pallas kernels for 0%

profile of v3, /device:TPU:38, one launch (start us, length us, event | category | flops | bytes accessed | tf_op | source)
XLA Modules:
  0.0 144.2 jit_solution(12840924897634666314)
XLA Ops:
  3.9 2.1 %convolution_convert_fusion.3 = bf16[256,256]{1,0:T(8,128)(2,1)S(1)} fusion(bf16[1,2560,256]{2,1,0:T(8,128)(2,1)} %param.7, bf16[256,1,2560]{2,0,1:T(8,128)(2,1)S(1)} %copy-done, f32[256]{0:T(256)S(1)} %bitcast.183, s32[256]{0:T(256)S(1)} %add.342), kind=kOutput, calls=%fused_computation.78 | convolution fusion | flops 369426432 | bytes 2754560 | tf_op jit(solution)/shard_map/dot_general | solution.py:90
  6.0 4.8 %collective-permute-start.3 = (bf16[256,256]{1,0:T(8,128)(2,1)S(1)}, bf16[256,256]{1,0:T(8,128)(2,1)S(1)}, u32[]{:S(2)}, u32[]{:S(2)}) collective-permute-start(bf16[256,256]{1,0:T(8,128)(2,1)S(1)} %convolution_convert_fusion.3), channel_id=1, source_target_pairs={{0,32},{32,64},{64,96},{96,128},{128,160},{160,192},{192,224},{1,3... | collective-permute-start | bytes 393224 | tf_op jit(solution)/shard_map/ppermute | solution.py:19
  15.1 8.4 %collective-permute-done = bf16[128,2560]{1,0:T(8,128)(2,1)} collective-permute-done((bf16[128,2560]{1,0:T(8,128)(2,1)S(1)}, bf16[128,2560]{1,0:T(8,128)(2,1)}, u32[]{:S(2)}, u32[]{:S(2)}) %collective-permute-start) | collective-permute-done | bytes 655392 | tf_op jit(solution)/shard_map/ppermute | solution.py:27
  25.5 2.0 %fusion.32 = f32[256,2560]{1,0:T(8,128)S(1)} fusion(bf16[256,256]{1,0:T(8,128)(2,1)S(1)} %collective-permute-done.3, bf16[1,4,256,2560]{3,2,1,0:T(8,128)(2,1)} %param.9), kind=kOutput, calls=%fused_computation.50 | convolution fusion | flops 335544320 | bytes 4063232 | tf_op jit(solution)/shard_map/dot_general | solution.py:95
  35.5 2.6 %convolution_convert_fusion.2 = bf16[256,256]{1,0:T(8,128)(2,1)S(1)} fusion(bf16[1,2560,256]{2,1,0:T(8,128)(2,1)} %param.7, bf16[128,2560]{1,0:T(8,128)(2,1)} %copy-done.3, bf16[128,2560]{1,0:T(8,128)(2,1)} %collective-permute-done, bf16[256,128]{1,0:T(8,128)(2,1)} %get-tuple-element.101, bf16[256,128]{1,0:T(8,128)(2,1)} %get-tuple-element.100, ...), kind=kOutput, calls=%fused_computation.77 | convolution fusion | flops 372441088 | bytes 2885633 | tf_op jit(solution)/shard_map/dot_general | solution.py:90
  38.1 6.5 %collective-permute-start.6 = (bf16[256,256]{1,0:T(8,128)(2,1)S(1)}, bf16[256,256]{1,0:T(8,128)(2,1)S(1)}, u32[]{:S(2)}, u32[]{:S(2)}) collective-permute-start(bf16[256,256]{1,0:T(8,128)(2,1)S(1)} %convolution_convert_fusion.2), channel_id=1, source_target_pairs={{0,32},{32,64},{64,96},{96,128},{128,160},{160,192},{192,224},{1,3... | collective-permute-start | bytes 393224 | tf_op jit(solution)/shard_map/ppermute | solution.py:19
  48.9 3.6 %collective-permute-done.7 = bf16[256,256]{1,0:T(8,128)(2,1)S(1)} collective-permute-done((bf16[256,256]{1,0:T(8,128)(2,1)S(1)}, bf16[256,256]{1,0:T(8,128)(2,1)S(1)}, u32[]{:S(2)}, u32[]{:S(2)}) %collective-permute-start.7) | collective-permute-done | bytes 131104 | tf_op jit(solution)/shard_map/ppermute | solution.py:19
  52.5 4.2 %collective-permute-done.8 = bf16[256,256]{1,0:T(8,128)(2,1)S(1)} collective-permute-done((bf16[256,256]{1,0:T(8,128)(2,1)S(1)}, bf16[256,256]{1,0:T(8,128)(2,1)S(1)}, u32[]{:S(2)}, u32[]{:S(2)}) %collective-permute-start.8) | collective-permute-done | bytes 131104 | tf_op jit(solution)/shard_map/ppermute | solution.py:19
  63.9 2.0 %collective-permute-start.12 = (bf16[64,2560]{1,0:T(8,128)(2,1)S(1)}, bf16[64,2560]{1,0:T(8,128)(2,1)S(1)}, u32[]{:S(2)}, u32[]{:S(2)}) collective-permute-start(bf16[64,2560]{1,0:T(8,128)(2,1)S(1)} %slice.198), channel_id=1, source_target_pairs={{0,4},{2,30},{4,8},{6,2},{8,12},{10,6},{12,16},{14,10},{16,20},{18... | collective-permute-start | bytes 983048 | tf_op jit(solution)/shard_map/ppermute | solution.py:35
  66.0 4.6 %collective-permute-start.13 = (bf16[16,2560]{1,0:T(8,128)(2,1)S(1)}, bf16[16,2560]{1,0:T(8,128)(2,1)S(1)}, u32[]{:S(2)}, u32[]{:S(2)}) collective-permute-start(bf16[16,2560]{1,0:T(8,128)(2,1)S(1)} %slice.199), channel_id=1, source_target_pairs={{0,8},{2,26},{4,12},{6,30},{8,16},{10,2},{12,20},{14,6},{16,24},{1... | collective-permute-start | bytes 245768 | tf_op jit(solution)/shard_map/ppermute | solution.py:35
  70.5 4.8 %collective-permute-done.13 = bf16[16,2560]{1,0:T(8,128)(2,1)S(1)} collective-permute-done((bf16[16,2560]{1,0:T(8,128)(2,1)S(1)}, bf16[16,2560]{1,0:T(8,128)(2,1)S(1)}, u32[]{:S(2)}, u32[]{:S(2)}) %collective-permute-start.13) | collective-permute-done | bytes 81952 | tf_op jit(solution)/shard_map/ppermute | solution.py:35
  77.0 6.0 %collective-permute-done.15 = bf16[32,2560]{1,0:T(8,128)(2,1)S(1)} collective-permute-done((bf16[32,2560]{1,0:T(8,128)(2,1)S(1)}, bf16[32,2560]{1,0:T(8,128)(2,1)S(1)}, u32[]{:S(2)}, u32[]{:S(2)}) %collective-permute-start.15) | collective-permute-done | bytes 163872 | tf_op jit(solution)/shard_map/ppermute | solution.py:35
  85.0 3.6 %collective-permute-start.17 = (bf16[32,2560]{1,0:T(8,128)(2,1)S(1)}, bf16[32,2560]{1,0:T(8,128)(2,1)S(1)}, u32[]{:S(2)}, u32[]{:S(2)}) collective-permute-start(bf16[32,2560]{1,0:T(8,128)(2,1)S(1)} %fusion.128), channel_id=1, source_target_pairs={{0,24},{2,10},{4,28},{6,14},{8,0},{10,18},{12,4},{14,22},{16,8},{1... | collective-permute-start | bytes 491528 | tf_op jit(solution)/shard_map/ppermute | solution.py:35
  88.6 2.9 %collective-permute-done.17 = bf16[32,2560]{1,0:T(8,128)(2,1)S(1)} collective-permute-done((bf16[32,2560]{1,0:T(8,128)(2,1)S(1)}, bf16[32,2560]{1,0:T(8,128)(2,1)S(1)}, u32[]{:S(2)}, u32[]{:S(2)}) %collective-permute-start.17) | collective-permute-done | bytes 163872 | tf_op jit(solution)/shard_map/ppermute | solution.py:35
  91.6 4.1 %collective-permute-start.18 = (bf16[64,2560]{1,0:T(8,128)(2,1)S(1)}, bf16[64,2560]{1,0:T(8,128)(2,1)S(1)}, u32[]{:S(2)}, u32[]{:S(2)}) collective-permute-start(bf16[64,2560]{1,0:T(8,128)(2,1)S(1)} %pad_maximum_fusion.4), channel_id=1, source_target_pairs={{0,28},{2,6},{4,0},{6,10},{8,4},{10,14},{12,8},{14,18},{16,12},{18... | collective-permute-start | bytes 983048 | tf_op jit(solution)/shard_map/ppermute | solution.py:35
  96.3 2.9 %collective-permute-start.19 = (bf16[16,2560]{1,0:T(8,128)(2,1)S(1)}, bf16[16,2560]{1,0:T(8,128)(2,1)S(1)}, u32[]{:S(2)}, u32[]{:S(2)}) collective-permute-start(bf16[16,2560]{1,0:T(8,128)(2,1)S(1)} %slice.180), channel_id=1, source_target_pairs={{0,24},{2,10},{4,28},{6,14},{8,0},{10,18},{12,4},{14,22},{16,8},{1... | collective-permute-start | bytes 245768 | tf_op jit(solution)/shard_map/ppermute | solution.py:35
  99.1 3.9 %collective-permute-done.19 = bf16[16,2560]{1,0:T(8,128)(2,1)S(1)} collective-permute-done((bf16[16,2560]{1,0:T(8,128)(2,1)S(1)}, bf16[16,2560]{1,0:T(8,128)(2,1)S(1)}, u32[]{:S(2)}, u32[]{:S(2)}) %collective-permute-start.19) | collective-permute-done | bytes 81952 | tf_op jit(solution)/shard_map/ppermute | solution.py:35
  103.1 2.8 %collective-permute-start.21 = (bf16[128,2560]{1,0:T(8,128)(2,1)S(1)}, bf16[128,2560]{1,0:T(8,128)(2,1)S(1)}, u32[]{:S(2)}, u32[]{:S(2)}) collective-permute-start(bf16[128,2560]{1,0:T(8,128)(2,1)S(1)} %pad_maximum_fusion), channel_id=1, source_target_pairs={{0,2},{2,0},{4,6},{6,4},{8,10},{10,8},{12,14},{14,12},{16,18},{18,... | collective-permute-start | bytes 1966088 | tf_op jit(solution)/shard_map/ppermute | solution.py:23
  109.9 4.6 %collective-permute-start.24 = (bf16[256,256]{1,0:T(8,128)(2,1)S(1)}, bf16[256,256]{1,0:T(8,128)(2,1)S(1)}, u32[]{:S(2)}, u32[]{:S(2)}) collective-permute-start(bf16[256,256]{1,0:T(8,128)(2,1)S(1)} %fusion.74), channel_id=1, source_target_pairs={{64,0},{96,32},{128,64},{160,96},{192,128},{224,160},{65,1},{97,33... | collective-permute-start | bytes 393224 | tf_op jit(solution)/shard_map/ppermute | solution.py:19
  115.1 2.3 %collective-permute-done.22 = bf16[80,2560]{1,0:T(8,128)(2,1)S(1)} collective-permute-done((bf16[80,2560]{1,0:T(8,128)(2,1)S(1)}, bf16[80,2560]{1,0:T(8,128)(2,1)S(1)}, u32[]{:S(2)}, u32[]{:S(2)}) %collective-permute-start.22) | collective-permute-done | bytes 409632 | tf_op jit(solution)/shard_map/ppermute | solution.py:27
  123.4 4.6 %collective-permute-start.26 = (bf16[512,256]{1,0:T(8,128)(2,1)S(1)}, bf16[512,256]{1,0:T(8,128)(2,1)S(1)}, u32[]{:S(2)}, u32[]{:S(2)}) collective-permute-start(bf16[512,256]{1,0:T(8,128)(2,1)S(1)} %pad_maximum_fusion.6), channel_id=1, source_target_pairs={{64,0},{96,32},{128,64},{160,96},{192,128},{224,160},{65,1},{97,33... | collective-permute-start | bytes 786440 | tf_op jit(solution)/shard_map/ppermute | solution.py:19
  128.0 2.1 %collective-permute-start.27 = (bf16[256,256]{1,0:T(8,128)(2,1)S(1)}, bf16[256,256]{1,0:T(8,128)(2,1)S(1)}, u32[]{:S(2)}, u32[]{:S(2)}) collective-permute-start(bf16[256,256]{1,0:T(8,128)(2,1)S(1)} %fusion.77), channel_id=1, source_target_pairs={{96,0},{128,32},{160,64},{192,96},{224,128},{97,1},{129,33},{161,6... | collective-permute-start | bytes 393224 | tf_op jit(solution)/shard_map/ppermute | solution.py:19
  130.2 2.1 %collective-permute-start.25 = (bf16[512,256]{1,0:T(8,128)(2,1)S(1)}, bf16[512,256]{1,0:T(8,128)(2,1)S(1)}, u32[]{:S(2)}, u32[]{:S(2)}) collective-permute-start(bf16[512,256]{1,0:T(8,128)(2,1)S(1)} %pad_maximum_fusion.5), channel_id=1, source_target_pairs={{32,0},{64,32},{96,64},{128,96},{160,128},{192,160},{224,192},{33,... | collective-permute-start | bytes 786440 | tf_op jit(solution)/shard_map/ppermute | solution.py:19
  137.4 5.2 %collective-permute-done.25 = bf16[512,256]{1,0:T(8,128)(2,1)S(1)} collective-permute-done((bf16[512,256]{1,0:T(8,128)(2,1)S(1)}, bf16[512,256]{1,0:T(8,128)(2,1)S(1)}, u32[]{:S(2)}, u32[]{:S(2)}) %collective-permute-start.25) | collective-permute-done | bytes 262176 | tf_op jit(solution)/shard_map/ppermute | solution.py:19
  (152 shorter events, 50.3 us)
Async XLA Ops:
  2.0 21.5 %collective-permute-start = (bf16[128,2560]{1,0:T(8,128)(2,1)S(1)}, bf16[128,2560]{1,0:T(8,128)(2,1)}, u32[]{:S(2)}, u32[]{:S(2)}) collective-permute-start(bf16[128,2560]{1,0:T(8,128)(2,1)S(1)} %dynamic-slice_bitcast_fusion), channel_id=1, source_target_pairs={{0,1},{1,0},{2,3},{3,2},{4,5},{5,4},{6,7},{7,6},{8,9},{9,8},{10,11... | collective-permute-start | bytes 1966088 | tf_op jit(solution)/shard_map/ppermute | solution.py:27
  6.0 19.4 %collective-permute-start.3 = (bf16[256,256]{1,0:T(8,128)(2,1)S(1)}, bf16[256,256]{1,0:T(8,128)(2,1)S(1)}, u32[]{:S(2)}, u32[]{:S(2)}) collective-permute-start(bf16[256,256]{1,0:T(8,128)(2,1)S(1)} %convolution_convert_fusion.3), channel_id=1, source_target_pairs={{0,32},{32,64},{64,96},{96,128},{128,160},{160,192},{192,224},{1,3... | collective-permute-start | bytes 393224 | tf_op jit(solution)/shard_map/ppermute | solution.py:19
  10.8 17.0 %collective-permute-start.4 = (bf16[256,256]{1,0:T(8,128)(2,1)S(1)}, bf16[256,256]{1,0:T(8,128)(2,1)S(1)}, u32[]{:S(2)}, u32[]{:S(2)}) collective-permute-start(bf16[256,256]{1,0:T(8,128)(2,1)S(1)} %convolution_convert_fusion.3), channel_id=1, source_target_pairs={{0,64},{32,96},{64,128},{96,160},{128,192},{160,224},{1,65},{33,97... | collective-permute-start | bytes 393224 | tf_op jit(solution)/shard_map/ppermute | solution.py:19
  12.1 17.5 %collective-permute-start.5 = (bf16[256,256]{1,0:T(8,128)(2,1)S(1)}, bf16[256,256]{1,0:T(8,128)(2,1)S(1)}, u32[]{:S(2)}, u32[]{:S(2)}) collective-permute-start(bf16[256,256]{1,0:T(8,128)(2,1)S(1)} %convolution_convert_fusion.3), channel_id=1, source_target_pairs={{0,96},{32,128},{64,160},{96,192},{128,224},{1,97},{33,129},{65,16... | collective-permute-start | bytes 393224 | tf_op jit(solution)/shard_map/ppermute | solution.py:19
  13.4 11.9 %collective-permute-start.1 = (bf16[16,2560]{1,0:T(8,128)(2,1)S(1)}, bf16[16,2560]{1,0:T(8,128)(2,1)S(1)}, u32[]{:S(2)}, u32[]{:S(2)}) collective-permute-start(bf16[16,2560]{1,0:T(8,128)(2,1)S(1)} %bitcast.182), channel_id=1, source_target_pairs={{16,0},{0,1},{17,2},{1,3},{18,4},{2,5},{19,6},{3,7},{20,8},{4,9},{... | collective-permute-start | bytes 245768 | tf_op jit(solution)/shard_map/ppermute | solution.py:45
  25.3 7.6 %collective-permute-start.2 = (bf16[128,2560]{1,0:T(8,128)(2,1)}, bf16[128,2560]{1,0:T(8,128)(2,1)S(1)}, u32[]{:S(2)}, u32[]{:S(2)}) collective-permute-start(bf16[128,2560]{1,0:T(8,128)(2,1)} %collective-permute-done), channel_id=1, source_target_pairs={{0,2},{2,0},{4,6},{6,4},{8,10},{10,8},{12,14},{14,12},{16,18},{18,... | collective-permute-start | bytes 1966088 | tf_op jit(solution)/shard_map/ppermute | solution.py:23
  33.8 22.8 %collective-permute-start.10 = (bf16[80,2560]{1,0:T(8,128)(2,1)S(1)}, bf16[80,2560]{1,0:T(8,128)(2,1)S(1)}, u32[]{:S(2)}, u32[]{:S(2)}) collective-permute-start(bf16[80,2560]{1,0:T(8,128)(2,1)S(1)} %slice.193), channel_id=1, source_target_pairs={{0,1},{1,0},{2,3},{3,2},{4,5},{5,4},{6,7},{7,6},{8,9},{9,8},{10,11... | collective-permute-start | bytes 1228808 | tf_op jit(solution)/shard_map/ppermute | solution.py:27
  38.1 10.8 %collective-permute-start.6 = (bf16[256,256]{1,0:T(8,128)(2,1)S(1)}, bf16[256,256]{1,0:T(8,128)(2,1)S(1)}, u32[]{:S(2)}, u32[]{:S(2)}) collective-permute-start(bf16[256,256]{1,0:T(8,128)(2,1)S(1)} %convolution_convert_fusion.2), channel_id=1, source_target_pairs={{0,32},{32,64},{64,96},{96,128},{128,160},{160,192},{192,224},{1,3... | collective-permute-start | bytes 393224 | tf_op jit(solution)/shard_map/ppermute | solution.py:19
  44.5 7.9 %collective-permute-start.7 = (bf16[256,256]{1,0:T(8,128)(2,1)S(1)}, bf16[256,256]{1,0:T(8,128)(2,1)S(1)}, u32[]{:S(2)}, u32[]{:S(2)}) collective-permute-start(bf16[256,256]{1,0:T(8,128)(2,1)S(1)} %convolution_convert_fusion.2), channel_id=1, source_target_pairs={{0,64},{32,96},{64,128},{96,160},{128,192},{160,224},{1,65},{33,97... | collective-permute-start | bytes 393224 | tf_op jit(solution)/shard_map/ppermute | solution.py:19
  45.8 10.8 %collective-permute-start.8 = (bf16[256,256]{1,0:T(8,128)(2,1)S(1)}, bf16[256,256]{1,0:T(8,128)(2,1)S(1)}, u32[]{:S(2)}, u32[]{:S(2)}) collective-permute-start(bf16[256,256]{1,0:T(8,128)(2,1)S(1)} %convolution_convert_fusion.2), channel_id=1, source_target_pairs={{0,96},{32,128},{64,160},{96,192},{128,224},{1,97},{33,129},{65,16... | collective-permute-start | bytes 393224 | tf_op jit(solution)/shard_map/ppermute | solution.py:19
  61.8 8.7 %collective-permute-start.14 = (bf16[48,2560]{1,0:T(8,128)(2,1)S(1)}, bf16[48,2560]{1,0:T(8,128)(2,1)S(1)}, u32[]{:S(2)}, u32[]{:S(2)}) collective-permute-start(bf16[48,2560]{1,0:T(8,128)(2,1)S(1)} %slice.200), channel_id=1, source_target_pairs={{0,1},{1,0},{2,3},{3,2},{4,5},{5,4},{6,7},{7,6},{8,9},{9,8},{10,11... | collective-permute-start | bytes 737288 | tf_op jit(solution)/shard_map/ppermute | solution.py:27
  63.9 11.4 %collective-permute-start.12 = (bf16[64,2560]{1,0:T(8,128)(2,1)S(1)}, bf16[64,2560]{1,0:T(8,128)(2,1)S(1)}, u32[]{:S(2)}, u32[]{:S(2)}) collective-permute-start(bf16[64,2560]{1,0:T(8,128)(2,1)S(1)} %slice.198), channel_id=1, source_target_pairs={{0,4},{2,30},{4,8},{6,2},{8,12},{10,6},{12,16},{14,10},{16,20},{18... | collective-permute-start | bytes 983048 | tf_op jit(solution)/shard_map/ppermute | solution.py:35
  66.0 9.3 %collective-permute-start.13 = (bf16[16,2560]{1,0:T(8,128)(2,1)S(1)}, bf16[16,2560]{1,0:T(8,128)(2,1)S(1)}, u32[]{:S(2)}, u32[]{:S(2)}) collective-permute-start(bf16[16,2560]{1,0:T(8,128)(2,1)S(1)} %slice.199), channel_id=1, source_target_pairs={{0,8},{2,26},{4,12},{6,30},{8,16},{10,2},{12,20},{14,6},{16,24},{1... | collective-permute-start | bytes 245768 | tf_op jit(solution)/shard_map/ppermute | solution.py:35
  75.5 7.6 %collective-permute-start.15 = (bf16[32,2560]{1,0:T(8,128)(2,1)S(1)}, bf16[32,2560]{1,0:T(8,128)(2,1)S(1)}, u32[]{:S(2)}, u32[]{:S(2)}) collective-permute-start(bf16[32,2560]{1,0:T(8,128)(2,1)S(1)} %pad_maximum_fusion.8), channel_id=1, source_target_pairs={{0,8},{2,26},{4,12},{6,30},{8,16},{10,2},{12,20},{14,6},{16,24},{1... | collective-permute-start | bytes 491528 | tf_op jit(solution)/shard_map/ppermute | solution.py:35
  85.0 6.6 %collective-permute-start.17 = (bf16[32,2560]{1,0:T(8,128)(2,1)S(1)}, bf16[32,2560]{1,0:T(8,128)(2,1)S(1)}, u32[]{:S(2)}, u32[]{:S(2)}) collective-permute-start(bf16[32,2560]{1,0:T(8,128)(2,1)S(1)} %fusion.128), channel_id=1, source_target_pairs={{0,24},{2,10},{4,28},{6,14},{8,0},{10,18},{12,4},{14,22},{16,8},{1... | collective-permute-start | bytes 491528 | tf_op jit(solution)/shard_map/ppermute | solution.py:35
  91.6 11.4 %collective-permute-start.18 = (bf16[64,2560]{1,0:T(8,128)(2,1)S(1)}, bf16[64,2560]{1,0:T(8,128)(2,1)S(1)}, u32[]{:S(2)}, u32[]{:S(2)}) collective-permute-start(bf16[64,2560]{1,0:T(8,128)(2,1)S(1)} %pad_maximum_fusion.4), channel_id=1, source_target_pairs={{0,28},{2,6},{4,0},{6,10},{8,4},{10,14},{12,8},{14,18},{16,12},{18... | collective-permute-start | bytes 983048 | tf_op jit(solution)/shard_map/ppermute | solution.py:35
  95.7 7.3 %collective-permute-start.20 = (bf16[48,2560]{1,0:T(8,128)(2,1)S(1)}, bf16[48,2560]{1,0:T(8,128)(2,1)S(1)}, u32[]{:S(2)}, u32[]{:S(2)}) collective-permute-start(bf16[48,2560]{1,0:T(8,128)(2,1)S(1)} %pad_maximum_fusion.7), channel_id=1, source_target_pairs={{0,1},{1,0},{2,3},{3,2},{4,5},{5,4},{6,7},{7,6},{8,9},{9,8},{10,11... | collective-permute-start | bytes 737288 | tf_op jit(solution)/shard_map/ppermute | solution.py:27
  96.3 6.7 %collective-permute-start.19 = (bf16[16,2560]{1,0:T(8,128)(2,1)S(1)}, bf16[16,2560]{1,0:T(8,128)(2,1)S(1)}, u32[]{:S(2)}, u32[]{:S(2)}) collective-permute-start(bf16[16,2560]{1,0:T(8,128)(2,1)S(1)} %slice.180), channel_id=1, source_target_pairs={{0,24},{2,10},{4,28},{6,14},{8,0},{10,18},{12,4},{14,22},{16,8},{1... | collective-permute-start | bytes 245768 | tf_op jit(solution)/shard_map/ppermute | solution.py:35
  103.1 4.5 %collective-permute-start.21 = (bf16[128,2560]{1,0:T(8,128)(2,1)S(1)}, bf16[128,2560]{1,0:T(8,128)(2,1)S(1)}, u32[]{:S(2)}, u32[]{:S(2)}) collective-permute-start(bf16[128,2560]{1,0:T(8,128)(2,1)S(1)} %pad_maximum_fusion), channel_id=1, source_target_pairs={{0,2},{2,0},{4,6},{6,4},{8,10},{10,8},{12,14},{14,12},{16,18},{18,... | collective-permute-start | bytes 1966088 | tf_op jit(solution)/shard_map/ppermute | solution.py:23
  105.9 11.5 %collective-permute-start.22 = (bf16[80,2560]{1,0:T(8,128)(2,1)S(1)}, bf16[80,2560]{1,0:T(8,128)(2,1)S(1)}, u32[]{:S(2)}, u32[]{:S(2)}) collective-permute-start(bf16[80,2560]{1,0:T(8,128)(2,1)S(1)} %pad_maximum_fusion.2), channel_id=1, source_target_pairs={{0,1},{1,0},{2,3},{3,2},{4,5},{5,4},{6,7},{7,6},{8,9},{9,8},{10,11... | collective-permute-start | bytes 1228808 | tf_op jit(solution)/shard_map/ppermute | solution.py:27
  109.9 10.0 %collective-permute-start.24 = (bf16[256,256]{1,0:T(8,128)(2,1)S(1)}, bf16[256,256]{1,0:T(8,128)(2,1)S(1)}, u32[]{:S(2)}, u32[]{:S(2)}) collective-permute-start(bf16[256,256]{1,0:T(8,128)(2,1)S(1)} %fusion.74), channel_id=1, source_target_pairs={{64,0},{96,32},{128,64},{160,96},{192,128},{224,160},{65,1},{97,33... | collective-permute-start | bytes 393224 | tf_op jit(solution)/shard_map/ppermute | solution.py:19
  123.4 12.2 %collective-permute-start.26 = (bf16[512,256]{1,0:T(8,128)(2,1)S(1)}, bf16[512,256]{1,0:T(8,128)(2,1)S(1)}, u32[]{:S(2)}, u32[]{:S(2)}) collective-permute-start(bf16[512,256]{1,0:T(8,128)(2,1)S(1)} %pad_maximum_fusion.6), channel_id=1, source_target_pairs={{64,0},{96,32},{128,64},{160,96},{192,128},{224,160},{65,1},{97,33... | collective-permute-start | bytes 786440 | tf_op jit(solution)/shard_map/ppermute | solution.py:19
  128.0 9.4 %collective-permute-start.27 = (bf16[256,256]{1,0:T(8,128)(2,1)S(1)}, bf16[256,256]{1,0:T(8,128)(2,1)S(1)}, u32[]{:S(2)}, u32[]{:S(2)}) collective-permute-start(bf16[256,256]{1,0:T(8,128)(2,1)S(1)} %fusion.77), channel_id=1, source_target_pairs={{96,0},{128,32},{160,64},{192,96},{224,128},{97,1},{129,33},{161,6... | collective-permute-start | bytes 393224 | tf_op jit(solution)/shard_map/ppermute | solution.py:19
  130.2 12.5 %collective-permute-start.25 = (bf16[512,256]{1,0:T(8,128)(2,1)S(1)}, bf16[512,256]{1,0:T(8,128)(2,1)S(1)}, u32[]{:S(2)}, u32[]{:S(2)}) collective-permute-start(bf16[512,256]{1,0:T(8,128)(2,1)S(1)} %pad_maximum_fusion.5), channel_id=1, source_target_pairs={{32,0},{64,32},{96,64},{128,96},{160,128},{192,160},{224,192},{33,... | collective-permute-start | bytes 786440 | tf_op jit(solution)/shard_map/ppermute | solution.py:19
  (14 other events, 75.9 us)

commit v4 on v3

--- a/solution.py
+++ b/solution.py
@@ -86,7 +86,7 @@
 
     def encode(rows, place):
         preact = jnp.dot(rows, enc_weight, preferred_element_type=F32) + b_enc[0]
-        natural = jnp.maximum(preact, 0.0).astype(BF16)
+        natural = lax.optimization_barrier(jnp.maximum(preact, 0.0).astype(BF16))
         return jnp.dot(place, natural, preferred_element_type=F32).astype(BF16)
 
     def decode_rest(total, sources):
@@ -99,7 +99,9 @@
         return [latents] + [over_layers(latents, k) for k in range(1, reach_count)]
 
     cut = 3 * piece
-    near = spread(encode(x, shuffle))
+    near = encode(x, shuffle)
+    norms = jnp.sqrt(jnp.sum(jnp.square(after(weights, near).astype(F32)), axis=2) + EPSILON)
+    near = spread(after(near, norms))
     near[0], far_x0 = lax.optimization_barrier((near[0], far_x0))
     near_sum = jnp.dot(near[0], weights[0], preferred_element_type=F32)
     far_x0, near_sum, own_targets = lax.optimization_barrier((far_x0, near_sum, own_targets))
@@ -111,9 +113,8 @@
     from_dp2 = over_dp(near_part[:cut])
 
     far_x1 = after(far_x1, near_sum)
-    far = spread(encode(jnp.concatenate([far_x0, far_x1], axis=0), swapped))
-    norms = jnp.sqrt(jnp.sum(jnp.square(weights.astype(F32)), axis=2) + EPSILON)
-    *far, from_dp1, norms = lax.optimization_barrier((*far, from_dp1, norms))
+    far = spread(encode(lax.optimization_barrier(jnp.concatenate([far_x0, far_x1], axis=0)), swapped))
+    *far, from_dp1 = lax.optimization_barrier((*far, from_dp1))
     far_sum = jnp.dot(far[0], weights[0], preferred_element_type=F32)
     far_sum = decode_rest(far_sum, far)
     part = far_sum[:group] + over_core(far_sum[group:].astype(BF16)).astype(F32)

time: 146 us -> 142 us (0.973)
  matrix products: 24 us -> 19.5 us
  other arithmetic: 5.35 us -> 8.09 us
  starting transfers between devices: 58.7 us -> 56.8 us
    ppermute x5, waiting for transfers between devices: 10.7 us -> 5.37 us  [over_dp(): return lax.ppermute(block, 'dp', [(0, 1), (1, 0)])]
    dot_general x2, matrix products: 4.68 us -> 0.46 us  [encode(): return jnp.dot(place, natural, preferred_element_type=F32).astype(BF16)]
    ppermute x1, waiting for transfers between devices: 0.01 us -> 3.95 us  [to_owner(): return lax.ppermute(block, ('latent', 'dp'), route)]
    reduce_sum x1, other arithmetic: 1.09 us -> 3.73 us  [shards(): jnp.sum(jnp.square(after(weights, near).astype(F32)), axis=2) + EPSILON]
    dot_general x0 -> x2, matrix products: none -> 2.33 us  [encode(): preact = jnp.dot(rows, enc_weight, preferred_element_type=F32) + b_enc[0]]
    ppermute x6, waiting for transfers between devices: 4.26 us -> 6.03 us  [over_core(): return lax.ppermute(block, 'latent', [(i, i ^ 1) for i in range(Z * CORES)])]
    ppermute x5, starting transfers between devices: 4.73 us -> 3.25 us  [over_dp(): return lax.ppermute(block, 'dp', [(0, 1), (1, 0)])]
    unnamed x25 -> x35, local copies, waits for them, and re-layouts: 3.05 us -> 2.93 us
  transfers between devices with their start and end apart: 28 -> 28, of which waited for: 14 -> 16; matrix products, arithmetic and copies ran while one was open for 15% -> 14% of each run, Pallas kernels for 0% -> 0%
where the time goes in v4:
time: 142 us; the launch traced here: 141 us
  starting transfers between devices  56.8 us (40%)
  waiting for transfers between devices  49.3 us (35%)
  matrix products  19.5 us (14%)
  other arithmetic  8.09 us (6%)
  local copies, waits for them, and re-layouts  5.82 us (4%)
  between operations  1.52 us (1%)
    ppermute x10, starting transfers between devices, over_layers(): return lax.ppermute(block, 'layer', route)  29.5 us
    ppermute x6, starting transfers between devices, over_z(): return lax.ppermute(block, 'latent', route)  18.6 us
    ppermute x6, waiting for transfers between devices, over_z(): return lax.ppermute(block, 'latent', route)  17.6 us
    ppermute x10, waiting for transfers between devices, over_layers(): return lax.ppermute(block, 'layer', route)  16.4 us
    ppermute x6, waiting for transfers between devices, over_core(): return lax.ppermute(block, 'latent', [(i, i ^ 1) for i in range(Z * CORES)])  6.03 us
    ppermute x5, waiting for transfers between devices, over_dp(): return lax.ppermute(block, 'dp', [(0, 1), (1, 0)])  5.37 us
    dot_general x6, matrix products, decode_rest(): total = total + jnp.dot(source, weights[k], preferred_element_type=F32)  4.45 us
    dot_general x8, matrix products, back(): lax.dot_general(grad, weights[k], (((1,), (1,)), ((), ())), preferred_ele...  4.3 us
  transfers between devices with their start and end apart: 28, of which 16 were waited for; matrix products, arithmetic and copies ran while one was open for 14% of the time, Pallas kernels for 0%

profile of v4, /device:TPU:38, one launch (start us, length us, event | category | flops | bytes accessed | tf_op | source)
XLA Modules:
  0.0 141.1 jit_solution(68778273176258876)
XLA Ops:
  6.0 3.7 %multiply_reduce_fusion = f32[4,256]{1,0:T(4,128)S(1)} fusion(bf16[4,256,2560]{2,1,0:T(8,128)(2,1)} %bitcast.164), kind=kLoop, calls=%fused_computation | loop fusion | flops 7863296 | bytes 5246976 | tf_op jit(solution)/shard_map/reduce_sum | solution.py:103
  9.8 4.8 %collective-permute-start.3 = (bf16[256,256]{1,0:T(8,128)(2,1)S(1)}, bf16[256,256]{1,0:T(8,128)(2,1)S(1)}, u32[]{:S(2)}, u32[]{:S(2)}) collective-permute-start(bf16[256,256]{1,0:T(8,128)(2,1)S(1)} %convolution_convert_fusion.3), channel_id=1, source_target_pairs={{0,32},{32,64},{64,96},{96,128},{128,160},{160,192},{192,224},{1,3... | collective-permute-start | bytes 393224 | tf_op jit(solution)/shard_map/ppermute | solution.py:19
  20.2 3.9 %collective-permute-done.1 = bf16[16,2560]{1,0:T(8,128)(2,1)S(1)} collective-permute-done((bf16[16,2560]{1,0:T(8,128)(2,1)S(1)}, bf16[16,2560]{1,0:T(8,128)(2,1)S(1)}, u32[]{:S(2)}, u32[]{:S(2)}) %collective-permute-start.1) | collective-permute-done | bytes 81952 | tf_op jit(solution)/shard_map/ppermute | solution.py:45
  33.1 7.3 %collective-permute-start.6 = (bf16[256,256]{1,0:T(8,128)(2,1)S(1)}, bf16[256,256]{1,0:T(8,128)(2,1)S(1)}, u32[]{:S(2)}, u32[]{:S(2)}) collective-permute-start(bf16[256,256]{1,0:T(8,128)(2,1)S(1)} %convolution_convert_fusion.2), channel_id=1, source_target_pairs={{0,32},{32,64},{64,96},{96,128},{128,160},{160,192},{192,224},{1,3... | collective-permute-start | bytes 393224 | tf_op jit(solution)/shard_map/ppermute | solution.py:19
  44.7 3.6 %collective-permute-done.7 = bf16[256,256]{1,0:T(8,128)(2,1)S(1)} collective-permute-done((bf16[256,256]{1,0:T(8,128)(2,1)S(1)}, bf16[256,256]{1,0:T(8,128)(2,1)S(1)}, u32[]{:S(2)}, u32[]{:S(2)}) %collective-permute-start.7) | collective-permute-done | bytes 131104 | tf_op jit(solution)/shard_map/ppermute | solution.py:19
  48.3 4.4 %collective-permute-done.8 = bf16[256,256]{1,0:T(8,128)(2,1)S(1)} collective-permute-done((bf16[256,256]{1,0:T(8,128)(2,1)S(1)}, bf16[256,256]{1,0:T(8,128)(2,1)S(1)}, u32[]{:S(2)}, u32[]{:S(2)}) %collective-permute-start.8) | collective-permute-done | bytes 131104 | tf_op jit(solution)/shard_map/ppermute | solution.py:19
  52.7 2.0 %fusion.34 = f32[256,2560]{1,0:T(8,128)S(1)} fusion(bf16[256,256]{1,0:T(8,128)(2,1)S(1)} %convolution_convert_fusion.2, bf16[1,4,256,2560]{3,2,1,0:T(8,128)(2,1)} %param.9), kind=kOutput, calls=%fused_computation.53 | convolution fusion | flops 335544320 | bytes 4063232 | tf_op jit(solution)/shard_map/dot_general | solution.py:118
  54.7 1.9 %convolution_add_fusion.6 = f32[256,2560]{1,0:T(8,128)S(1)} fusion(f32[256,2560]{1,0:T(8,128)S(1)} %fusion.34, bf16[256,256]{1,0:T(8,128)(2,1)S(1)} %collective-permute-done.6, bf16[1,4,256,2560]{3,2,1,0:T(8,128)(2,1)} %param.9), kind=kOutput, calls=%fused_computation.7 | convolution fusion | flops 336199680 | bytes 6684672 | tf_op jit(solution)/shard_map/dot_general | solution.py:95
  60.2 2.0 %collective-permute-start.12 = (bf16[64,2560]{1,0:T(8,128)(2,1)S(1)}, bf16[64,2560]{1,0:T(8,128)(2,1)S(1)}, u32[]{:S(2)}, u32[]{:S(2)}) collective-permute-start(bf16[64,2560]{1,0:T(8,128)(2,1)S(1)} %slice.198), channel_id=1, source_target_pairs={{0,4},{2,30},{4,8},{6,2},{8,12},{10,6},{12,16},{14,10},{16,20},{18... | collective-permute-start | bytes 983048 | tf_op jit(solution)/shard_map/ppermute | solution.py:35
  62.3 4.6 %collective-permute-start.13 = (bf16[16,2560]{1,0:T(8,128)(2,1)S(1)}, bf16[16,2560]{1,0:T(8,128)(2,1)S(1)}, u32[]{:S(2)}, u32[]{:S(2)}) collective-permute-start(bf16[16,2560]{1,0:T(8,128)(2,1)S(1)} %slice.199), channel_id=1, source_target_pairs={{0,8},{2,26},{4,12},{6,30},{8,16},{10,2},{12,20},{14,6},{16,24},{1... | collective-permute-start | bytes 245768 | tf_op jit(solution)/shard_map/ppermute | solution.py:35
  66.8 4.8 %collective-permute-done.13 = bf16[16,2560]{1,0:T(8,128)(2,1)S(1)} collective-permute-done((bf16[16,2560]{1,0:T(8,128)(2,1)S(1)}, bf16[16,2560]{1,0:T(8,128)(2,1)S(1)}, u32[]{:S(2)}, u32[]{:S(2)}) %collective-permute-start.13) | collective-permute-done | bytes 81952 | tf_op jit(solution)/shard_map/ppermute | solution.py:35
  73.3 6.0 %collective-permute-done.15 = bf16[32,2560]{1,0:T(8,128)(2,1)S(1)} collective-permute-done((bf16[32,2560]{1,0:T(8,128)(2,1)S(1)}, bf16[32,2560]{1,0:T(8,128)(2,1)S(1)}, u32[]{:S(2)}, u32[]{:S(2)}) %collective-permute-start.15) | collective-permute-done | bytes 163872 | tf_op jit(solution)/shard_map/ppermute | solution.py:35
  81.3 3.6 %collective-permute-start.17 = (bf16[32,2560]{1,0:T(8,128)(2,1)S(1)}, bf16[32,2560]{1,0:T(8,128)(2,1)S(1)}, u32[]{:S(2)}, u32[]{:S(2)}) collective-permute-start(bf16[32,2560]{1,0:T(8,128)(2,1)S(1)} %fusion.111), channel_id=1, source_target_pairs={{0,24},{2,10},{4,28},{6,14},{8,0},{10,18},{12,4},{14,22},{16,8},{1... | collective-permute-start | bytes 491528 | tf_op jit(solution)/shard_map/ppermute | solution.py:35
  84.9 2.9 %collective-permute-done.17 = bf16[32,2560]{1,0:T(8,128)(2,1)S(1)} collective-permute-done((bf16[32,2560]{1,0:T(8,128)(2,1)S(1)}, bf16[32,2560]{1,0:T(8,128)(2,1)S(1)}, u32[]{:S(2)}, u32[]{:S(2)}) %collective-permute-start.17) | collective-permute-done | bytes 163872 | tf_op jit(solution)/shard_map/ppermute | solution.py:35
  87.9 4.1 %collective-permute-start.18 = (bf16[64,2560]{1,0:T(8,128)(2,1)S(1)}, bf16[64,2560]{1,0:T(8,128)(2,1)S(1)}, u32[]{:S(2)}, u32[]{:S(2)}) collective-permute-start(bf16[64,2560]{1,0:T(8,128)(2,1)S(1)} %pad_maximum_fusion.5), channel_id=1, source_target_pairs={{0,28},{2,6},{4,0},{6,10},{8,4},{10,14},{12,8},{14,18},{16,12},{18... | collective-permute-start | bytes 983048 | tf_op jit(solution)/shard_map/ppermute | solution.py:35
  92.6 2.9 %collective-permute-start.19 = (bf16[16,2560]{1,0:T(8,128)(2,1)S(1)}, bf16[16,2560]{1,0:T(8,128)(2,1)S(1)}, u32[]{:S(2)}, u32[]{:S(2)}) collective-permute-start(bf16[16,2560]{1,0:T(8,128)(2,1)S(1)} %slice.180), channel_id=1, source_target_pairs={{0,24},{2,10},{4,28},{6,14},{8,0},{10,18},{12,4},{14,22},{16,8},{1... | collective-permute-start | bytes 245768 | tf_op jit(solution)/shard_map/ppermute | solution.py:35
  95.5 3.8 %collective-permute-done.19 = bf16[16,2560]{1,0:T(8,128)(2,1)S(1)} collective-permute-done((bf16[16,2560]{1,0:T(8,128)(2,1)S(1)}, bf16[16,2560]{1,0:T(8,128)(2,1)S(1)}, u32[]{:S(2)}, u32[]{:S(2)}) %collective-permute-start.19) | collective-permute-done | bytes 81952 | tf_op jit(solution)/shard_map/ppermute | solution.py:35
  99.4 2.8 %collective-permute-start.21 = (bf16[128,2560]{1,0:T(8,128)(2,1)S(1)}, bf16[128,2560]{1,0:T(8,128)(2,1)S(1)}, u32[]{:S(2)}, u32[]{:S(2)}) collective-permute-start(bf16[128,2560]{1,0:T(8,128)(2,1)S(1)} %pad_maximum_fusion.1), channel_id=1, source_target_pairs={{0,2},{2,0},{4,6},{6,4},{8,10},{10,8},{12,14},{14,12},{16,18},{18,... | collective-permute-start | bytes 1966088 | tf_op jit(solution)/shard_map/ppermute | solution.py:23
  106.3 2.4 %collective-permute-start.24 = (bf16[256,256]{1,0:T(8,128)(2,1)S(1)}, bf16[256,256]{1,0:T(8,128)(2,1)S(1)}, u32[]{:S(2)}, u32[]{:S(2)}) collective-permute-start(bf16[256,256]{1,0:T(8,128)(2,1)S(1)} %fusion.77), channel_id=1, source_target_pairs={{64,0},{96,32},{128,64},{160,96},{192,128},{224,160},{65,1},{97,33... | collective-permute-start | bytes 393224 | tf_op jit(solution)/shard_map/ppermute | solution.py:19
  109.3 4.4 %collective-permute-done.22 = bf16[80,2560]{1,0:T(8,128)(2,1)S(1)} collective-permute-done((bf16[80,2560]{1,0:T(8,128)(2,1)S(1)}, bf16[80,2560]{1,0:T(8,128)(2,1)S(1)}, u32[]{:S(2)}, u32[]{:S(2)}) %collective-permute-start.22) | collective-permute-done | bytes 409632 | tf_op jit(solution)/shard_map/ppermute | solution.py:27
  119.8 2.5 %collective-permute-start.26 = (bf16[512,256]{1,0:T(8,128)(2,1)S(1)}, bf16[512,256]{1,0:T(8,128)(2,1)S(1)}, u32[]{:S(2)}, u32[]{:S(2)}) collective-permute-start(bf16[512,256]{1,0:T(8,128)(2,1)S(1)} %pad_maximum_fusion.7), channel_id=1, source_target_pairs={{64,0},{96,32},{128,64},{160,96},{192,128},{224,160},{65,1},{97,33... | collective-permute-start | bytes 786440 | tf_op jit(solution)/shard_map/ppermute | solution.py:19
  122.3 5.3 %collective-permute-start.27 = (bf16[256,256]{1,0:T(8,128)(2,1)S(1)}, bf16[256,256]{1,0:T(8,128)(2,1)S(1)}, u32[]{:S(2)}, u32[]{:S(2)}) collective-permute-start(bf16[256,256]{1,0:T(8,128)(2,1)S(1)} %fusion.80), channel_id=1, source_target_pairs={{96,0},{128,32},{160,64},{192,96},{224,128},{97,1},{129,33},{161,6... | collective-permute-start | bytes 393224 | tf_op jit(solution)/shard_map/ppermute | solution.py:19
  127.7 1.9 %collective-permute-start.25 = (bf16[512,256]{1,0:T(8,128)(2,1)S(1)}, bf16[512,256]{1,0:T(8,128)(2,1)S(1)}, u32[]{:S(2)}, u32[]{:S(2)}) collective-permute-start(bf16[512,256]{1,0:T(8,128)(2,1)S(1)} %pad_maximum_fusion.6), channel_id=1, source_target_pairs={{32,0},{64,32},{96,64},{128,96},{160,128},{192,160},{224,192},{33,... | collective-permute-start | bytes 786440 | tf_op jit(solution)/shard_map/ppermute | solution.py:19
  133.1 6.4 %collective-permute-done.25 = bf16[512,256]{1,0:T(8,128)(2,1)S(1)} collective-permute-done((bf16[512,256]{1,0:T(8,128)(2,1)S(1)}, bf16[512,256]{1,0:T(8,128)(2,1)S(1)}, u32[]{:S(2)}, u32[]{:S(2)}) %collective-permute-start.25) | collective-permute-done | bytes 262176 | tf_op jit(solution)/shard_map/ppermute | solution.py:19
  (164 shorter events, 47.3 us)
Async XLA Ops:
  2.0 17.7 %collective-permute-start = (bf16[128,2560]{1,0:T(8,128)(2,1)S(1)}, bf16[128,2560]{1,0:T(8,128)(2,1)S(1)}, u32[]{:S(2)}, u32[]{:S(2)}) collective-permute-start(bf16[128,2560]{1,0:T(8,128)(2,1)S(1)} %dynamic-slice_bitcast_fusion), channel_id=1, source_target_pairs={{0,1},{1,0},{2,3},{3,2},{4,5},{5,4},{6,7},{7,6},{8,9},{9,8},{10,11... | collective-permute-start | bytes 1966088 | tf_op jit(solution)/shard_map/ppermute | solution.py:27
  9.8 14.9 %collective-permute-start.3 = (bf16[256,256]{1,0:T(8,128)(2,1)S(1)}, bf16[256,256]{1,0:T(8,128)(2,1)S(1)}, u32[]{:S(2)}, u32[]{:S(2)}) collective-permute-start(bf16[256,256]{1,0:T(8,128)(2,1)S(1)} %convolution_convert_fusion.3), channel_id=1, source_target_pairs={{0,32},{32,64},{64,96},{96,128},{128,160},{160,192},{192,224},{1,3... | collective-permute-start | bytes 393224 | tf_op jit(solution)/shard_map/ppermute | solution.py:19
  14.6 10.9 %collective-permute-start.4 = (bf16[256,256]{1,0:T(8,128)(2,1)S(1)}, bf16[256,256]{1,0:T(8,128)(2,1)S(1)}, u32[]{:S(2)}, u32[]{:S(2)}) collective-permute-start(bf16[256,256]{1,0:T(8,128)(2,1)S(1)} %convolution_convert_fusion.3), channel_id=1, source_target_pairs={{0,64},{32,96},{64,128},{96,160},{128,192},{160,224},{1,65},{33,97... | collective-permute-start | bytes 393224 | tf_op jit(solution)/shard_map/ppermute | solution.py:19
  15.9 10.8 %collective-permute-start.5 = (bf16[256,256]{1,0:T(8,128)(2,1)S(1)}, bf16[256,256]{1,0:T(8,128)(2,1)S(1)}, u32[]{:S(2)}, u32[]{:S(2)}) collective-permute-start(bf16[256,256]{1,0:T(8,128)(2,1)S(1)} %convolution_convert_fusion.3), channel_id=1, source_target_pairs={{0,96},{32,128},{64,160},{96,192},{128,224},{1,97},{33,129},{65,16... | collective-permute-start | bytes 393224 | tf_op jit(solution)/shard_map/ppermute | solution.py:19
  17.2 7.0 %collective-permute-start.1 = (bf16[16,2560]{1,0:T(8,128)(2,1)S(1)}, bf16[16,2560]{1,0:T(8,128)(2,1)S(1)}, u32[]{:S(2)}, u32[]{:S(2)}) collective-permute-start(bf16[16,2560]{1,0:T(8,128)(2,1)S(1)} %bitcast.179), channel_id=1, source_target_pairs={{16,0},{0,1},{17,2},{1,3},{18,4},{2,5},{19,6},{3,7},{20,8},{4,9},{... | collective-permute-start | bytes 245768 | tf_op jit(solution)/shard_map/ppermute | solution.py:45
  24.2 5.2 %collective-permute-start.2 = (bf16[128,2560]{1,0:T(8,128)(2,1)S(1)}, bf16[128,2560]{1,0:T(8,128)(2,1)S(1)}, u32[]{:S(2)}, u32[]{:S(2)}) collective-permute-start(bf16[128,2560]{1,0:T(8,128)(2,1)S(1)} %collective-permute-done), channel_id=1, source_target_pairs={{0,2},{2,0},{4,6},{6,4},{8,10},{10,8},{12,14},{14,12},{16,18},{18,... | collective-permute-start | bytes 1966088 | tf_op jit(solution)/shard_map/ppermute | solution.py:23
  32.2 20.5 %collective-permute-start.10 = (bf16[80,2560]{1,0:T(8,128)(2,1)}, bf16[80,2560]{1,0:T(8,128)(2,1)S(1)}, u32[]{:S(2)}, u32[]{:S(2)}) collective-permute-start(bf16[80,2560]{1,0:T(8,128)(2,1)} %slice.193), channel_id=1, source_target_pairs={{0,1},{1,0},{2,3},{3,2},{4,5},{5,4},{6,7},{7,6},{8,9},{9,8},{10,11... | collective-permute-start | bytes 1228808 | tf_op jit(solution)/shard_map/ppermute | solution.py:27
  33.1 11.6 %collective-permute-start.6 = (bf16[256,256]{1,0:T(8,128)(2,1)S(1)}, bf16[256,256]{1,0:T(8,128)(2,1)S(1)}, u32[]{:S(2)}, u32[]{:S(2)}) collective-permute-start(bf16[256,256]{1,0:T(8,128)(2,1)S(1)} %convolution_convert_fusion.2), channel_id=1, source_target_pairs={{0,32},{32,64},{64,96},{96,128},{128,160},{160,192},{192,224},{1,3... | collective-permute-start | bytes 393224 | tf_op jit(solution)/shard_map/ppermute | solution.py:19
  40.4 7.9 %collective-permute-start.7 = (bf16[256,256]{1,0:T(8,128)(2,1)S(1)}, bf16[256,256]{1,0:T(8,128)(2,1)S(1)}, u32[]{:S(2)}, u32[]{:S(2)}) collective-permute-start(bf16[256,256]{1,0:T(8,128)(2,1)S(1)} %convolution_convert_fusion.2), channel_id=1, source_target_pairs={{0,64},{32,96},{64,128},{96,160},{128,192},{160,224},{1,65},{33,97... | collective-permute-start | bytes 393224 | tf_op jit(solution)/shard_map/ppermute | solution.py:19
  41.7 11.0 %collective-permute-start.8 = (bf16[256,256]{1,0:T(8,128)(2,1)S(1)}, bf16[256,256]{1,0:T(8,128)(2,1)S(1)}, u32[]{:S(2)}, u32[]{:S(2)}) collective-permute-start(bf16[256,256]{1,0:T(8,128)(2,1)S(1)} %convolution_convert_fusion.2), channel_id=1, source_target_pairs={{0,96},{32,128},{64,160},{96,192},{128,224},{1,97},{33,129},{65,16... | collective-permute-start | bytes 393224 | tf_op jit(solution)/shard_map/ppermute | solution.py:19
  58.1 8.7 %collective-permute-start.14 = (bf16[48,2560]{1,0:T(8,128)(2,1)S(1)}, bf16[48,2560]{1,0:T(8,128)(2,1)S(1)}, u32[]{:S(2)}, u32[]{:S(2)}) collective-permute-start(bf16[48,2560]{1,0:T(8,128)(2,1)S(1)} %slice.200), channel_id=1, source_target_pairs={{0,1},{1,0},{2,3},{3,2},{4,5},{5,4},{6,7},{7,6},{8,9},{9,8},{10,11... | collective-permute-start | bytes 737288 | tf_op jit(solution)/shard_map/ppermute | solution.py:27
  60.2 11.4 %collective-permute-start.12 = (bf16[64,2560]{1,0:T(8,128)(2,1)S(1)}, bf16[64,2560]{1,0:T(8,128)(2,1)S(1)}, u32[]{:S(2)}, u32[]{:S(2)}) collective-permute-start(bf16[64,2560]{1,0:T(8,128)(2,1)S(1)} %slice.198), channel_id=1, source_target_pairs={{0,4},{2,30},{4,8},{6,2},{8,12},{10,6},{12,16},{14,10},{16,20},{18... | collective-permute-start | bytes 983048 | tf_op jit(solution)/shard_map/ppermute | solution.py:35
  62.3 9.3 %collective-permute-start.13 = (bf16[16,2560]{1,0:T(8,128)(2,1)S(1)}, bf16[16,2560]{1,0:T(8,128)(2,1)S(1)}, u32[]{:S(2)}, u32[]{:S(2)}) collective-permute-start(bf16[16,2560]{1,0:T(8,128)(2,1)S(1)} %slice.199), channel_id=1, source_target_pairs={{0,8},{2,26},{4,12},{6,30},{8,16},{10,2},{12,20},{14,6},{16,24},{1... | collective-permute-start | bytes 245768 | tf_op jit(solution)/shard_map/ppermute | solution.py:35
  71.8 7.6 %collective-permute-start.15 = (bf16[32,2560]{1,0:T(8,128)(2,1)S(1)}, bf16[32,2560]{1,0:T(8,128)(2,1)S(1)}, u32[]{:S(2)}, u32[]{:S(2)}) collective-permute-start(bf16[32,2560]{1,0:T(8,128)(2,1)S(1)} %pad_maximum_fusion.9), channel_id=1, source_target_pairs={{0,8},{2,26},{4,12},{6,30},{8,16},{10,2},{12,20},{14,6},{16,24},{1... | collective-permute-start | bytes 491528 | tf_op jit(solution)/shard_map/ppermute | solution.py:35
  81.3 6.6 %collective-permute-start.17 = (bf16[32,2560]{1,0:T(8,128)(2,1)S(1)}, bf16[32,2560]{1,0:T(8,128)(2,1)S(1)}, u32[]{:S(2)}, u32[]{:S(2)}) collective-permute-start(bf16[32,2560]{1,0:T(8,128)(2,1)S(1)} %fusion.111), channel_id=1, source_target_pairs={{0,24},{2,10},{4,28},{6,14},{8,0},{10,18},{12,4},{14,22},{16,8},{1... | collective-permute-start | bytes 491528 | tf_op jit(solution)/shard_map/ppermute | solution.py:35
  87.9 11.4 %collective-permute-start.18 = (bf16[64,2560]{1,0:T(8,128)(2,1)S(1)}, bf16[64,2560]{1,0:T(8,128)(2,1)S(1)}, u32[]{:S(2)}, u32[]{:S(2)}) collective-permute-start(bf16[64,2560]{1,0:T(8,128)(2,1)S(1)} %pad_maximum_fusion.5), channel_id=1, source_target_pairs={{0,28},{2,6},{4,0},{6,10},{8,4},{10,14},{12,8},{14,18},{16,12},{18... | collective-permute-start | bytes 983048 | tf_op jit(solution)/shard_map/ppermute | solution.py:35
  92.0 7.3 %collective-permute-start.20 = (bf16[48,2560]{1,0:T(8,128)(2,1)S(1)}, bf16[48,2560]{1,0:T(8,128)(2,1)S(1)}, u32[]{:S(2)}, u32[]{:S(2)}) collective-permute-start(bf16[48,2560]{1,0:T(8,128)(2,1)S(1)} %pad_maximum_fusion.8), channel_id=1, source_target_pairs={{0,1},{1,0},{2,3},{3,2},{4,5},{5,4},{6,7},{7,6},{8,9},{9,8},{10,11... | collective-permute-start | bytes 737288 | tf_op jit(solution)/shard_map/ppermute | solution.py:27
  92.6 6.7 %collective-permute-start.19 = (bf16[16,2560]{1,0:T(8,128)(2,1)S(1)}, bf16[16,2560]{1,0:T(8,128)(2,1)S(1)}, u32[]{:S(2)}, u32[]{:S(2)}) collective-permute-start(bf16[16,2560]{1,0:T(8,128)(2,1)S(1)} %slice.180), channel_id=1, source_target_pairs={{0,24},{2,10},{4,28},{6,14},{8,0},{10,18},{12,4},{14,22},{16,8},{1... | collective-permute-start | bytes 245768 | tf_op jit(solution)/shard_map/ppermute | solution.py:35
  99.4 4.6 %collective-permute-start.21 = (bf16[128,2560]{1,0:T(8,128)(2,1)S(1)}, bf16[128,2560]{1,0:T(8,128)(2,1)S(1)}, u32[]{:S(2)}, u32[]{:S(2)}) collective-permute-start(bf16[128,2560]{1,0:T(8,128)(2,1)S(1)} %pad_maximum_fusion.1), channel_id=1, source_target_pairs={{0,2},{2,0},{4,6},{6,4},{8,10},{10,8},{12,14},{14,12},{16,18},{18,... | collective-permute-start | bytes 1966088 | tf_op jit(solution)/shard_map/ppermute | solution.py:23
  102.2 11.5 %collective-permute-start.22 = (bf16[80,2560]{1,0:T(8,128)(2,1)S(1)}, bf16[80,2560]{1,0:T(8,128)(2,1)S(1)}, u32[]{:S(2)}, u32[]{:S(2)}) collective-permute-start(bf16[80,2560]{1,0:T(8,128)(2,1)S(1)} %pad_maximum_fusion.3), channel_id=1, source_target_pairs={{0,1},{1,0},{2,3},{3,2},{4,5},{5,4},{6,7},{7,6},{8,9},{9,8},{10,11... | collective-permute-start | bytes 1228808 | tf_op jit(solution)/shard_map/ppermute | solution.py:27
  106.3 10.0 %collective-permute-start.24 = (bf16[256,256]{1,0:T(8,128)(2,1)S(1)}, bf16[256,256]{1,0:T(8,128)(2,1)S(1)}, u32[]{:S(2)}, u32[]{:S(2)}) collective-permute-start(bf16[256,256]{1,0:T(8,128)(2,1)S(1)} %fusion.77), channel_id=1, source_target_pairs={{64,0},{96,32},{128,64},{160,96},{192,128},{224,160},{65,1},{97,33... | collective-permute-start | bytes 393224 | tf_op jit(solution)/shard_map/ppermute | solution.py:19
  119.8 13.3 %collective-permute-start.26 = (bf16[512,256]{1,0:T(8,128)(2,1)S(1)}, bf16[512,256]{1,0:T(8,128)(2,1)S(1)}, u32[]{:S(2)}, u32[]{:S(2)}) collective-permute-start(bf16[512,256]{1,0:T(8,128)(2,1)S(1)} %pad_maximum_fusion.7), channel_id=1, source_target_pairs={{64,0},{96,32},{128,64},{160,96},{192,128},{224,160},{65,1},{97,33... | collective-permute-start | bytes 786440 | tf_op jit(solution)/shard_map/ppermute | solution.py:19
  122.3 10.8 %collective-permute-start.27 = (bf16[256,256]{1,0:T(8,128)(2,1)S(1)}, bf16[256,256]{1,0:T(8,128)(2,1)S(1)}, u32[]{:S(2)}, u32[]{:S(2)}) collective-permute-start(bf16[256,256]{1,0:T(8,128)(2,1)S(1)} %fusion.80), channel_id=1, source_target_pairs={{96,0},{128,32},{160,64},{192,96},{224,128},{97,1},{129,33},{161,6... | collective-permute-start | bytes 393224 | tf_op jit(solution)/shard_map/ppermute | solution.py:19
  127.7 11.8 %collective-permute-start.25 = (bf16[512,256]{1,0:T(8,128)(2,1)S(1)}, bf16[512,256]{1,0:T(8,128)(2,1)S(1)}, u32[]{:S(2)}, u32[]{:S(2)}) collective-permute-start(bf16[512,256]{1,0:T(8,128)(2,1)S(1)} %pad_maximum_fusion.6), channel_id=1, source_target_pairs={{32,0},{64,32},{96,64},{128,96},{160,128},{192,160},{224,192},{33,... | collective-permute-start | bytes 786440 | tf_op jit(solution)/shard_map/ppermute | solution.py:19
  (19 other events, 104.5 us)
